TPU v7x, 32 devices: a whole 2x2x4 slice. The times are simulated.
32 devices in a mesh: batch: 8 (over y, x, core), seq: 4 (over z).
Axes of the slice: x: 2, y: 2, z: 4, core: 2. Of those that a mesh axis runs over, the one named last changes fastest.
Arguments:
- hidden_in: bfloat16 [32, 512, 768], P('batch', 'seq'), may hold values from -6 to 6
- lengths: int32 [32], P('batch'), may hold values from 64 to 512, as said below
- w_qkv: bfloat16 [768, 2304], replicated, may hold values from -0.21875 to 0.21875
- b_q: bfloat16 [768], replicated, may hold values from -3 to 3
- b_v: bfloat16 [768], replicated, may hold values from -3 to 3
- w_o: bfloat16 [768, 768], replicated, may hold values from -2.5 to 2.5
- b_o: bfloat16 [768], replicated, may hold values from -3 to 3
- gain_one: bfloat16 [768], replicated, may hold values from 0.25 to 1.75
- shift_one: bfloat16 [768], replicated, may hold values from -3 to 3
- w_in: bfloat16 [768, 3072], replicated, may hold values from -0.21875 to 0.21875
- b_in: bfloat16 [3072], replicated, may hold values from -3 to 3
- w_out: bfloat16 [3072, 768], replicated, may hold values from -0.109375 to 0.109375
- b_out: bfloat16 [768], replicated, may hold values from -3 to 3
- gain_two: bfloat16 [768], replicated, may hold values from 0.25 to 1.75
- shift_two: bfloat16 [768], replicated, may hold values from -3 to 3
- cot_hidden: bfloat16 [32, 512, 768], P('batch', 'seq'), may hold values from -6 to 6
- cot_pooled: bfloat16 [32, 768], P('batch'), may hold values from -24 to 24
Outputs:
- out_hidden: bfloat16 [32, 512, 768], P('batch', 'seq')
- pooled: float32 [32, 768], P('batch')
- grad_in: bfloat16 [32, 512, 768], P('batch', 'seq')
- grad_w_qkv: float32 [768, 2304], P('batch', 'seq')
- grad_b_q: float32 [768], replicated
- grad_b_v: float32 [768], replicated
- grad_w_o: float32 [768, 768], P('batch', 'seq')
- grad_b_o: float32 [768], replicated
- grad_gain_one: float32 [768], replicated
- grad_shift_one: float32 [768], replicated
- grad_w_in: float32 [768, 3072], P('batch', 'seq')
- grad_b_in: float32 [3072], replicated
- grad_w_out: float32 [3072, 768], P('batch', 'seq')
- grad_b_out: float32 [768], replicated
- grad_gain_two: float32 [768], replicated
- grad_shift_two: float32 [768], replicated
Inputs may be any that keep to these rules, and one draw needn't show every extreme that they name: `lengths`: of the 4 passages of each index of batch, one is at full length 512.
All inputs are finite; a program needn't handle non-finite values.
Results may differ from a plain program's by a relative error of at most 0.019.
Values may be sent and summed in bfloat16 or wider, within the bound.
A program may use at most 128 MiB of HBM per device.

v0:
```python
import jax
import jax.numpy as jnp
from jax import lax
from jax.sharding import PartitionSpec as P

H = 12


def layer_norm(values):
    centre_val = jnp.mean(values, -1, keepdims=True)
    centred = values - centre_val
    inv_std = lax.rsqrt(jnp.mean(centred * centred, -1, keepdims=True) + 1e-12)
    return (centred * inv_std, inv_std)


def norm_back(grad_normed, normed, inv_std):
    first_mean = jnp.mean(grad_normed, -1, keepdims=True)
    second_mean = jnp.mean(grad_normed * normed, -1, keepdims=True)
    return inv_std * (grad_normed - first_mean - normed * second_mean)


def gelu_slope(pre_act):
    cumulative = 0.5 * (1.0 + lax.erf(pre_act * 0.7071067811865476))
    density = jnp.exp(-0.5 * pre_act * pre_act) * 0.3989422804014327
    return cumulative + pre_act * density


def ffn_front(middle_low, w_in, b_in):
    pre_act = jnp.dot(middle_low, w_in, preferred_element_type=jnp.float32) + b_in.astype(
        jnp.float32
    )
    act_low = jax.nn.gelu(pre_act, approximate=False).astype(jnp.bfloat16)
    return (pre_act, act_low)


def run_layer(hidden_in, lengths, cot_hidden, cot_pooled, weights):
    (
        w_qkv,
        b_q,
        b_v,
        w_o,
        b_o,
        gain_one,
        shift_one,
        w_in,
        b_in,
        w_out,
        b_out,
        gain_two,
        shift_two,
    ) = weights
    seqs_here, block_len, model_width = hidden_in.shape
    head_count = H
    head_size = model_width // head_count
    score_scale = head_size ** (-0.5)
    row_count = seqs_here * block_len
    flat_rows = hidden_in.reshape(row_count, model_width)
    bias_all = jnp.concatenate(
        [b_q.astype(jnp.float32), jnp.zeros((model_width,), jnp.float32), b_v.astype(jnp.float32)]
    )
    projected = jnp.dot(flat_rows, w_qkv, preferred_element_type=jnp.float32) + bias_all
    queries = (
        projected[:, :model_width]
        .astype(jnp.bfloat16)
        .reshape(seqs_here, block_len, head_count, head_size)
    )
    local_kv = (
        projected[:, model_width:]
        .astype(jnp.bfloat16)
        .reshape(seqs_here, block_len, 2 * model_width)
    )
    whole_kv = lax.all_gather(local_kv, "seq", axis=1, tiled=True)
    start_pos = lax.axis_index("seq") * block_len
    seq_len = whole_kv.shape[1]
    keys_all = whole_kv[:, :, :model_width].reshape(seqs_here, seq_len, head_count, head_size)
    values_all = whole_kv[:, :, model_width:].reshape(seqs_here, seq_len, head_count, head_size)
    key_live = jnp.arange(seq_len, dtype=jnp.int32)[None, :] < lengths[:, None]
    scores = (
        jnp.einsum("sqhd,skhd->shqk", queries, keys_all, preferred_element_type=jnp.float32)
        * score_scale
    )
    scores = jnp.where(key_live[:, None, None, :], scores, -1e30)
    row_max = jnp.max(scores, -1, keepdims=True)
    expo_vals = jnp.exp(scores - row_max)
    probs = expo_vals / jnp.sum(expo_vals, -1, keepdims=True)
    probs_low = probs.astype(jnp.bfloat16)
    mixed = jnp.einsum("shqk,skhd->sqhd", probs_low, values_all, preferred_element_type=jnp.float32)
    attended = mixed.reshape(row_count, model_width).astype(jnp.bfloat16)
    branch = jnp.dot(attended, w_o, preferred_element_type=jnp.float32) + b_o.astype(jnp.float32)
    normed_one, inv_one = layer_norm(flat_rows.astype(jnp.float32) + branch)
    middle = normed_one * gain_one.astype(jnp.float32) + shift_one.astype(jnp.float32)
    middle_low = middle.astype(jnp.bfloat16)
    pre_act, act_low = ffn_front(middle_low, w_in, b_in)
    ffn_out = jnp.dot(act_low, w_out, preferred_element_type=jnp.float32) + b_out.astype(
        jnp.float32
    )
    normed_two, inv_two = layer_norm(middle + ffn_out)
    output_rows = normed_two * gain_two.astype(jnp.float32) + shift_two.astype(jnp.float32)
    out_hidden = output_rows.astype(jnp.bfloat16).reshape(seqs_here, block_len, model_width)
    query_pos = start_pos + jnp.arange(block_len, dtype=jnp.int32)
    query_live = (query_pos[None, :] < lengths[:, None]).astype(jnp.float32)
    pooled_part = jnp.sum(
        output_rows.reshape(seqs_here, block_len, model_width) * query_live[:, :, None], 1
    )
    counts = lengths.astype(jnp.float32)[:, None]
    pooled = lax.psum(pooled_part, "seq") / counts
    pooled_grad = cot_pooled.astype(jnp.float32) / counts
    grad_final = cot_hidden.astype(jnp.float32) + query_live[:, :, None] * pooled_grad[:, None, :]
    grad_final = grad_final.reshape(row_count, model_width)
    grad_gain_two = jnp.sum(grad_final * normed_two, 0)
    grad_shift_two = jnp.sum(grad_final, 0)
    grad_second = norm_back(grad_final * gain_two.astype(jnp.float32), normed_two, inv_two)
    grad_ffn = grad_second.astype(jnp.bfloat16)
    grad_b_out = jnp.sum(grad_ffn.astype(jnp.float32), 0)
    pre_again, act_again = (pre_act, act_low)
    grad_w_out = jnp.einsum("rf,rd->fd", act_again, grad_ffn, preferred_element_type=jnp.float32)
    grad_act = jnp.einsum("rd,fd->rf", grad_ffn, w_out, preferred_element_type=jnp.float32).astype(
        jnp.bfloat16
    )
    grad_pre = (grad_act.astype(jnp.float32) * gelu_slope(pre_again)).astype(jnp.bfloat16)
    grad_b_in = jnp.sum(grad_pre.astype(jnp.float32), 0)
    grad_w_in = jnp.einsum("rd,rf->df", middle_low, grad_pre, preferred_element_type=jnp.float32)
    grad_middle = grad_second + jnp.einsum(
        "rf,df->rd", grad_pre, w_in, preferred_element_type=jnp.float32
    )
    grad_gain_one = jnp.sum(grad_middle * normed_one, 0)
    grad_shift_one = jnp.sum(grad_middle, 0)
    grad_first = norm_back(grad_middle * gain_one.astype(jnp.float32), normed_one, inv_one)
    grad_branch = grad_first.astype(jnp.bfloat16)
    grad_b_o = jnp.sum(grad_branch.astype(jnp.float32), 0)
    grad_w_o = jnp.einsum("rc,rd->cd", attended, grad_branch, preferred_element_type=jnp.float32)
    grad_att = jnp.einsum("rd,cd->rc", grad_branch, w_o, preferred_element_type=jnp.float32).astype(
        jnp.bfloat16
    )
    grad_att = grad_att.reshape(seqs_here, block_len, head_count, head_size)
    grad_probs = jnp.einsum(
        "sqhd,skhd->shqk", grad_att, values_all, preferred_element_type=jnp.float32
    )
    inner_sum = jnp.sum(probs * grad_probs, -1, keepdims=True)
    grad_scores = (probs * (grad_probs - inner_sum)).astype(jnp.bfloat16)
    grad_query = (
        jnp.einsum("shqk,skhd->sqhd", grad_scores, keys_all, preferred_element_type=jnp.float32)
        * score_scale
    )
    grad_query = grad_query.astype(jnp.bfloat16).reshape(row_count, model_width)
    grad_keys = (
        jnp.einsum("shqk,sqhd->skhd", grad_scores, queries, preferred_element_type=jnp.float32)
        * score_scale
    )
    grad_values = jnp.einsum(
        "shqk,sqhd->skhd", probs_low, grad_att, preferred_element_type=jnp.float32
    )
    grad_kv = jnp.concatenate(
        [
            grad_keys.reshape(seqs_here, seq_len, model_width),
            grad_values.reshape(seqs_here, seq_len, model_width),
        ],
        -1,
    )
    grad_kv = lax.psum_scatter(
        grad_kv.astype(jnp.bfloat16), "seq", scatter_dimension=1, tiled=True
    ).astype(jnp.float32)
    grad_kv = grad_kv.astype(jnp.bfloat16).reshape(row_count, 2 * model_width)
    grad_proj = jnp.concatenate([grad_query, grad_kv], 1)
    grad_b_q = jnp.sum(grad_query.astype(jnp.float32), 0)
    grad_b_v = jnp.sum(grad_kv[:, model_width:].astype(jnp.float32), 0)
    grad_w_qkv = jnp.einsum("rd,rc->dc", flat_rows, grad_proj, preferred_element_type=jnp.float32)
    grad_in = (
        jnp.einsum("rc,dc->rd", grad_proj, w_qkv, preferred_element_type=jnp.float32) + grad_first
    )
    grad_in = grad_in.astype(jnp.bfloat16).reshape(seqs_here, block_len, model_width)
    matrices = (grad_w_qkv, grad_w_o, grad_w_in, grad_w_out)
    vectors = (
        grad_b_q,
        grad_b_v,
        grad_b_o,
        grad_gain_one,
        grad_shift_one,
        grad_b_in,
        grad_b_out,
        grad_gain_two,
        grad_shift_two,
    )
    return (out_hidden, pooled, grad_in, matrices, vectors)


def body(
    hidden_in,
    lengths,
    w_qkv,
    b_q,
    b_v,
    w_o,
    b_o,
    gain_one,
    shift_one,
    w_in,
    b_in,
    w_out,
    b_out,
    gain_two,
    shift_two,
    cot_hidden,
    cot_pooled,
):
    weights = (
        w_qkv,
        b_q,
        b_v,
        w_o,
        b_o,
        gain_one,
        shift_one,
        w_in,
        b_in,
        w_out,
        b_out,
        gain_two,
        shift_two,
    )
    out_hidden, pooled, grad_in, matrices, vectors = run_layer(
        hidden_in, lengths, cot_hidden, cot_pooled, weights
    )
    matrices = (
        lax.psum_scatter(matrices[0], "batch", scatter_dimension=0, tiled=True),
        lax.psum_scatter(matrices[1], "batch", scatter_dimension=0, tiled=True),
        lax.psum_scatter(matrices[2], "batch", scatter_dimension=0, tiled=True),
        lax.psum_scatter(matrices[3], "batch", scatter_dimension=0, tiled=True),
    )
    matrices = (
        lax.psum_scatter(
            matrices[0].astype(jnp.bfloat16), "seq", scatter_dimension=1, tiled=True
        ).astype(jnp.float32),
        lax.psum_scatter(
            matrices[1].astype(jnp.bfloat16), "seq", scatter_dimension=1, tiled=True
        ).astype(jnp.float32),
        lax.psum_scatter(
            matrices[2].astype(jnp.bfloat16), "seq", scatter_dimension=1, tiled=True
        ).astype(jnp.float32),
        lax.psum_scatter(
            matrices[3].astype(jnp.bfloat16), "seq", scatter_dimension=1, tiled=True
        ).astype(jnp.float32),
    )
    vectors = lax.psum(
        (
            vectors[0],
            vectors[1],
            vectors[2],
            vectors[3],
            vectors[4],
            vectors[5],
            vectors[6],
            vectors[7],
            vectors[8],
        ),
        ("batch", "seq"),
    )
    return (
        out_hidden,
        pooled,
        grad_in,
        matrices[0],
        vectors[0],
        vectors[1],
        matrices[1],
        vectors[2],
        vectors[3],
        vectors[4],
        matrices[2],
        vectors[5],
        matrices[3],
        vectors[6],
        vectors[7],
        vectors[8],
    )


def solution(mesh):
    in_specs = (
        P("batch", "seq", None),
        P("batch"),
        P(),
        P(),
        P(),
        P(),
        P(),
        P(),
        P(),
        P(),
        P(),
        P(),
        P(),
        P(),
        P(),
        P("batch", "seq", None),
        P("batch", None),
    )
    out_specs = (
        P("batch", "seq", None),
        P("batch", None),
        P("batch", "seq", None),
        P("batch", "seq"),
        P(),
        P(),
        P("batch", "seq"),
        P(),
        P(),
        P(),
        P("batch", "seq"),
        P(),
        P("batch", "seq"),
        P(),
        P(),
        P(),
    )
    return jax.shard_map(body, mesh=mesh, in_specs=in_specs, out_specs=out_specs, check_vma=False)
```

profile of v0, /device:TPU:0, one launch (start us, length us, event | category | flops | bytes accessed | tf_op | source)
XLA Modules:
  0.0 745.0 jit_solution(16428491593159704054)
XLA Ops:
  32.4 100.9 %all-gather.2.cloned.1.call-done = bf16[4,512,1536]{2,1,0:T(8,128)(2,1)} async-done(((bf16[4,128,1536]{2,1,0:T(8,128)(2,1)}), bf16[4,512,1536]{2,1,0:T(8,128)(2,1)}) %all-gather.2.cloned.1.call-update) | async-done | bytes 6291472 | tf_op jit(solution)/shard_map/all_gather | solution.py:72
  133.3 5.9 fusion.71
  139.3 4.7 copy.58
  143.9 4.9 copy.56
  148.8 11.5 %fusion.72 = (f32[4,12,128]{2,1,0:T(8,128)}, f32[4,12,128,512]{3,2,1,0:T(8,128)}) fusion(pred[4,512]{1,0:T(4,128)(4,1)S(1)} %copy-done.30, bf16[4,512,12,64]{1,3,2,0:T(8,128)(2,1)} %bitcast.81, bf16[4,128,12,64]{1,0,3,2:T(4,128)(2,1)} %reshape.193), kind=kOutput, calls=%fused_computation.123 | convolution fusion | flops 415236608 | bytes 16541696 | tf_op jit(solution)/shard_map/sub | solution.py:84
  160.3 8.0 %fusion.35 = bf16[4,128,12,64]{1,3,2,0:T(8,128)(2,1)S(1)} fusion(bf16[4,512,12,64]{1,3,2,0:T(8,128)(2,1)} %bitcast.89, f32[4,12,128,512]{3,2,1,0:T(8,128)} %get-tuple-element.91, f32[4,12,128]{2,1,0:T(8,128)} %get-tuple-element.90), kind=kOutput, calls=%fused_computation.80 | convolution fusion | flops 409337856 | bytes 16539648 | tf_op jit(solution)/shard_map/shqk,skhd->sqhd/dot_general | solution.py:87
  170.3 19.1 %fusion.4 = (bf16[512,3072]{1,0:T(8,128)(2,1)S(1)}, f32[512,3072]{1,0:T(8,128)S(1)}) fusion(f32[3072]{0:T(1024)S(1)} %copy-done.22, bf16[768,3072]{1,0:T(8,128)(2,1)} %param.26, f32[512,768]{1,0:T(8,128)S(1)} %get-tuple-element.93, f32[768]{0:T(1024)S(1)} %copy-done.26, f32[768]{0:T(1024)S(1)} %convert_element_type.152, f32[512]{0:T(512)S(1)} %add_rsqrt_fusion.1, ...), kind=kOutput, calls=%fused_computation.10 | convolution fusion | flops 2521694208 | bytes 15751168 | tf_op jit(solution)/shard_map/dot_general | solution.py:29
  189.6 3.2 fusion.78
  197.7 5.3 convert_reduce_fusion
  203.0 3.7 multiply_reduce_fusion.1
  215.6 13.2 %multiply_reduce_fusion = (f32[4,12,128]{2,1,0:T(8,128)S(1)}, f32[4,12,128,512]{3,2,1,0:T(8,128)}) fusion(f32[4,12,128,512]{3,2,1,0:T(8,128)} %get-tuple-element.91, f32[4,12,128]{2,1,0:T(8,128)} %get-tuple-element.90, bf16[4,512,12,64]{1,3,2,0:T(8,128)(2,1)} %bitcast.90, bf16[4,128,12,64]{1,0,3,2:T(4,128)(2,1)} %reshape.198), kind=kOutput, calls=%fused_computation.2 | convolution fusion | flops 412084224 | bytes 29147136 | tf_op jit(solution)/shard_map/sqhd,skhd->shqk/dot_general | solution.py:136
  228.8 6.7 fusion.26
  235.5 6.1 multiply_convert_fusion
  245.4 4.6 copy.66
  250.0 4.7 copy.67
  254.7 6.0 pad_maximum_fusion
  260.8 3.9 fusion.41
  264.7 9.4 %fusion.62 = f32[3072,768]{1,0:T(8,128)} fusion(bf16[512,3072]{1,0:T(8,128)(2,1)} %copy-done.5, f32[512,768]{1,0:T(8,128)} %copy-done.2), kind=kOutput, calls=%fused_computation.115 | convolution fusion | flops 2416312320 | bytes 14155776 | tf_op jit(solution)/shard_map/rf,rd->fd/dot_general | solution.py:116
  274.8 8.9 %fusion.67 = f32[768,3072]{1,0:T(8,128)} fusion(bf16[512,3072]{1,0:T(8,128)(2,1)} %copy-done.33, f32[512,768]{1,0:T(8,128)} %copy-done.3, f32[768]{0:T(1024)} %convert_element_type.153, f32[768]{0:T(1024)} %copy-done.15, f32[512]{0:T(512)} %copy-done.23, f32[512]{0:T(512)S(1)} %copy-done.14), kind=kOutput, calls=%fused_computation.120 | convolution fusion | flops 2417885184 | bytes 14166016 | tf_op jit(solution)/shard_map/rd,rf->df/dot_general | solution.py:122
  283.8 6.8 convert_reduce_fusion.4
  294.6 75.3 %reduce-scatter.16.cloned.1.call-done = bf16[4,128,1536]{2,1,0:T(8,128)(2,1)} async-done(((bf16[4,512,1536]{2,1,0:T(8,128)(2,1)}), bf16[4,128,1536]{2,1,0:T(8,128)(2,1)}) %reduce-scatter.16.cloned.1.call-update) | async-done | bytes 1572880 | tf_op jit(solution)/shard_map/reduce_scatter | solution.py:160
  369.8 6.8 convolution_bitcast_fusion
  376.6 8.2 %copy.71 = f32[768,2304]{1,0:T(8,128)} copy(f32[768,2304]{0,1:T(8,128)} %convolution_bitcast_fusion) | data formatting | bytes 14155776
  384.8 31.4 %reduce-scatter.20.cloned.1.call-done = f32[96,768]{1,0:T(8,128)} async-done(((f32[768,768]{1,0:T(8,128)}), f32[96,768]{1,0:T(8,128)}) %reduce-scatter.20.cloned.1.call-update) | async-done | bytes 294928 | tf_op jit(solution)/shard_map/reduce_scatter | solution.py:226
  419.7 76.9 %reduce-scatter.26.cloned.1.call-done = f32[384,768]{1,0:T(8,128)} async-done(((f32[3072,768]{1,0:T(8,128)}), f32[384,768]{1,0:T(8,128)}) %reduce-scatter.26.cloned.1.call-update) | async-done | bytes 1179664 | tf_op jit(solution)/shard_map/reduce_scatter | solution.py:228
  500.9 75.9 %reduce-scatter.22.cloned.1.call-done = f32[96,3072]{1,0:T(8,128)} async-done(((f32[768,3072]{1,0:T(8,128)}), f32[96,3072]{1,0:T(8,128)}) %reduce-scatter.22.cloned.1.call-update) | async-done | bytes 1179664 | tf_op jit(solution)/shard_map/reduce_scatter | solution.py:227
  580.4 19.2 %psum.70 = f32[4,768]{1,0:T(4,128)} all-reduce(f32[4,768]{1,0:T(4,128)S(1)} %get-tuple-element.72), channel_id=1, replica_groups=mesh['batch'=8,'seq'=4] {'seq'}, use_global_device_ids=true, to_apply=%region_7.8 | all-reduce | flops 3072 | bytes 24576 | tf_op jit(solution)/shard_map/psum | solution.py:106
  599.6 46.5 %reduce-scatter.28.cloned.1.call-done = f32[96,2304]{1,0:T(8,128)} async-done(((f32[768,2304]{1,0:T(8,128)}), f32[96,2304]{1,0:T(8,128)}) %reduce-scatter.28.cloned.1.call-update) | async-done | bytes 884752
  649.8 18.5 %reduce-scatter.30.cloned.1.call-done = bf16[192,96]{1,0:T(8,128)(2,1)} async-done(((bf16[768,96]{1,0:T(8,128)(2,1)}), bf16[192,96]{1,0:T(8,128)(2,1)}) %reduce-scatter.30.cloned.1.call-update) | async-done | bytes 36880
  673.1 40.6 %all-reduce = (f32[768]{0:T(1024)}, f32[768]{0:T(1024)}, f32[768]{0:T(1024)}, f32[768]{0:T(1024)}, f32[768]{0:T(1024)}, /*index=5*/f32[3072]{0:T(1024)}, f32[768]{0:T(1024)}, f32[768]{0:T(1024)}, f32[768]{0:T(1024)}) all-reduce(f32[768]{0:T(1024)} %reduce_sum.194, ...), channel_id=1, replica_groups=mesh['batch'=8,'seq'=4] {'batch','seq'}, use_global_device_ids=true, to_apply=%region_17.18 | all-reduce | flops 9216 | bytes 73728 | tf_op jit(solution)/shard_map/psum | solution.py:244
  713.7 5.0 add_convert_fusion
  723.9 12.4 %reduce-scatter.18.cloned.1.call-done = bf16[96,576]{0,1:T(8,128)(2,1)} async-done(((bf16[96,2304]{0,1:T(8,128)(2,1)}), bf16[96,576]{0,1:T(8,128)(2,1)}) %reduce-scatter.18.cloned.1.call-update) | async-done | bytes 110608 | tf_op jit(solution)/shard_map/reduce_scatter | solution.py:231
  (165 shorter events, 76.1 us)
Async XLA Ops:
  7.2 126.1 %all-gather.2.cloned.1.call-start = ((), (), s32[]{:S(2)}) async-start(), calls=%async_computation.9 | async-start | bytes 7864320 | tf_op jit(solution)/shard_map/all_gather | solution.py:72
  15.1 6.9 copy-start.28
  15.1 9.4 %copy-start.25 = (bf16[3072]{0:T(1024)(128)(2,1)S(1)}, bf16[3072]{0:T(1024)(128)(2,1)}, u32[]{:S(2)}) copy-start(bf16[3072]{0:T(1024)(128)(2,1)} %param.27) | copy-start | bytes 18436
  15.1 354.7 %reduce-scatter.16.cloned.1.call-start = ((), (), s32[]{:S(2)}) async-start(), calls=%async_computation.10 | async-start | bytes 7864320 | tf_op jit(solution)/shard_map/reduce_scatter | solution.py:160
  23.2 166.3 %copy-start.15 = (f32[768]{0:T(1024)}, f32[768]{0:T(1024)S(1)}, u32[]{:S(2)}) copy-start(f32[768]{0:T(1024)S(1)} %convert_element_type.152) | copy-start | bytes 9220
  27.2 112.1 %copy-start.29 = (f32[4]{0:T(128)}, f32[4]{0:T(128)S(1)}, u32[]{:S(2)}) copy-start(f32[4]{0:T(128)S(1)} %convert_element_type.162) | copy-start | bytes 52
  160.3 8.6 %copy-start.27 = (f32[768]{0:T(1024)S(1)}, f32[768]{0:T(1024)}, u32[]{:S(2)}) copy-start(f32[768]{0:T(1024)} %convert_element_type.151) | copy-start | bytes 9220
  160.3 8.6 %copy-start.31 = (bf16[768,768]{1,0:T(8,128)(2,1)S(1)}, bf16[768,768]{1,0:T(8,128)(2,1)}, u32[]{:S(2)}) copy-start(bf16[768,768]{1,0:T(8,128)(2,1)} %param.22) | copy-start | bytes 3538948
  160.3 8.7 %copy-start.32 = (bf16[4,128,768]{2,1,0:T(8,128)(2,1)S(1)}, bf16[4,128,768]{2,1,0:T(8,128)(2,1)}, u32[]{:S(2)}) copy-start(bf16[4,128,768]{2,1,0:T(8,128)(2,1)} %param.17) | copy-start | bytes 2359300
  169.0 20.5 %slice-start.3 = ((s8[4718592]{0:T(1024)(128)(4,1)}), s8[4194304]{0:T(1024)(128)(4,1)S(1)}, s32[]{:S(2)}) async-start(s8[4718592]{0:T(1024)(128)(4,1)} %bitcast.102), calls=%async_computation.22 | async-start | bytes 8388608
  170.0 36.7 %copy-start.3 = (f32[512,768]{1,0:T(8,128)}, f32[512,768]{1,0:T(8,128)S(1)}, u32[]{:S(2)}) copy-start(f32[512,768]{1,0:T(8,128)S(1)} %get-tuple-element.93) | copy-start | bytes 4718596
  170.0 36.7 %copy-start.13 = (f32[512]{0:T(512)}, f32[512]{0:T(512)S(1)}, u32[]{:S(2)}) copy-start(f32[512]{0:T(512)S(1)} %broadcast_multiply_fusion.4) | copy-start | bytes 6148
  170.3 36.4 %copy-start.23 = (f32[512]{0:T(512)}, f32[512]{0:T(512)S(1)}, u32[]{:S(2)}) copy-start(f32[512]{0:T(512)S(1)} %add_rsqrt_fusion.1) | copy-start | bytes 6148
  170.3 19.2 %slice-start.4 = ((s8[4718592]{0:T(1024)(128)(4,1)}), s8[524288]{0:T(1024)(128)(4,1)S(1)}, s32[]{:S(2)}) async-start(s8[4718592]{0:T(1024)(128)(4,1)} %bitcast.102), calls=%async_computation.23 | async-start | bytes 1048576
  196.6 6.4 slice-start.5
  215.6 13.2 %copy-start.10 = (bf16[4,128,12,64]{1,0,3,2:T(4,128)(2,1)S(1)}, bf16[4,128,12,64]{1,0,3,2:T(4,128)(2,1)}, u32[]{:S(2)}) copy-start(bf16[4,128,12,64]{1,0,3,2:T(4,128)(2,1)} %reshape.198) | copy-start | bytes 2359300
  215.6 13.2 %copy-start.12 = (f32[4,12,128]{2,1,0:T(8,128)S(1)}, f32[4,12,128]{2,1,0:T(8,128)}, u32[]{:S(2)}) copy-start(f32[4,12,128]{2,1,0:T(8,128)} %get-tuple-element.90) | copy-start | bytes 73732
  215.6 19.9 %slice-start = ((s8[12582912]{0:T(1024)(128)(4,1)}), s8[4194304]{0:T(1024)(128)(4,1)S(1)}, s32[]{:S(2)}) async-start(s8[12582912]{0:T(1024)(128)(4,1)} %bitcast.84), calls=%async_computation.19 | async-start | bytes 8388608
  215.6 19.9 %slice-start.1 = ((s8[12582912]{0:T(1024)(128)(4,1)}), s8[4194304]{0:T(1024)(128)(4,1)S(1)}, s32[]{:S(2)}) async-start(s8[12582912]{0:T(1024)(128)(4,1)} %bitcast.84), calls=%async_computation.20 | async-start | bytes 8388608
  228.8 6.8 slice-start.2
  260.7 155.5 %reduce-scatter.20.cloned.1.call-start = ((), (), s32[]{:S(2)}) async-start(), calls=%async_computation.12 | async-start | bytes 2654208 | tf_op jit(solution)/shard_map/reduce_scatter | solution.py:226
  264.7 231.8 %reduce-scatter.26.cloned.1.call-start = ((), (), s32[]{:S(2)}) async-start(), calls=%async_computation.15 | async-start | bytes 10616832 | tf_op jit(solution)/shard_map/reduce_scatter | solution.py:228
  274.2 302.6 %reduce-scatter.22.cloned.1.call-start = ((), (), s32[]{:S(2)}) async-start(), calls=%async_computation.13 | async-start | bytes 10616832 | tf_op jit(solution)/shard_map/reduce_scatter | solution.py:227
  283.8 362.3 %reduce-scatter.28.cloned.1.call-start = ((), (), s32[]{:S(2)}) async-start(), calls=%async_computation.16 | async-start | bytes 7962624
  384.8 283.5 %reduce-scatter.30.cloned.1.call-start = ((), (), s32[]{:S(2)}) async-start(), calls=%async_computation.17 | async-start | bytes 245760
  419.6 299.1 %reduce-scatter.32.cloned.1.call-start = ((), (), s32[]{:S(2)}) async-start(), calls=%async_computation.18 | async-start | bytes 737280
  500.8 172.3 %copy-start.18 = (f32[768]{0:T(1024)S(1)}, f32[768]{0:T(1024)}, u32[]{:S(2)}) copy-start(f32[768]{0:T(1024)} %get-tuple-element.70) | copy-start | bytes 9220
  500.8 221.4 %reduce-scatter.24.cloned.1.call-start = ((), (), s32[]{:S(2)}) async-start(), calls=%async_computation.14 | async-start | bytes 737280 | tf_op jit(solution)/shard_map/reduce_scatter | solution.py:237
  579.0 157.3 %reduce-scatter.18.cloned.1.call-start = ((), (), s32[]{:S(2)}) async-start(), calls=%async_computation.11 | async-start | bytes 737280 | tf_op jit(solution)/shard_map/reduce_scatter | solution.py:231
  599.6 73.5 %copy-start.19 = (f32[768]{0:T(1024)S(1)}, f32[768]{0:T(1024)}, u32[]{:S(2)}) copy-start(f32[768]{0:T(1024)} %get-tuple-element.64) | copy-start | bytes 9220
  599.6 73.5 %copy-start.20 = (f32[768]{0:T(1024)S(1)}, f32[768]{0:T(1024)}, u32[]{:S(2)}) copy-start(f32[768]{0:T(1024)} %get-tuple-element.82) | copy-start | bytes 9220
  599.6 73.5 %copy-start.21 = (f32[768]{0:T(1024)S(1)}, f32[768]{0:T(1024)}, u32[]{:S(2)}) copy-start(f32[768]{0:T(1024)} %get-tuple-element.84) | copy-start | bytes 9220
  (19 other events, 61.0 us)
Sparse Core Ops, SparseCore 0:
  15.2 118.0 all-gather.1
  260.8 108.9 reduce-scatter.15
  373.2 42.9 reduce-scatter.19
  420.0 76.4 reduce-scatter.25
  500.3 76.4 reduce-scatter.21
  580.6 65.4 reduce-scatter.27
  648.9 19.3 reduce-scatter.29
  670.7 20.1 reduce-scatter.31
  693.3 20.2 reduce-scatter.23
  715.8 20.4 reduce-scatter.17
where the time goes:
time: 750 us; the launch traced here: 745 us
  waiting for transfers between devices  438 us (58%)
  matrix products  120 us (16%)
  local copies, waits for them, and re-layouts  68.6 us (9%)
  blocking collectives  59.8 us (8%)
  other arithmetic  42.8 us (6%)
  between operations  14.9 us (2%)
    all_gather x1, waiting for transfers between devices, run_layer(): whole_kv = lax.all_gather(local_kv, 'seq', axis=1, tiled=True)  101 us
    reduce_scatter x1, waiting for transfers between devices, body(): lax.psum_scatter(matrices[3], 'batch', scatter_dimension=0, tiled=True)  76.9 us
    reduce_scatter x1, waiting for transfers between devices, body(): lax.psum_scatter(matrices[2], 'batch', scatter_dimension=0, tiled=True)  75.9 us
    reduce_scatter x1, waiting for transfers between devices, run_layer(): lax.psum_scatter(grad_kv.astype(jnp.bfloat16), 'seq', scatter_dimension=1...  75.3 us
    unnamed x13, waiting for transfers between devices  65.2 us
    psum x1, blocking collectives, body(): lax.psum((vectors[0], vectors[1], vectors[2], vectors[3], vectors[4], vec...  40.6 us
    reduce_scatter x1, waiting for transfers between devices, body(): lax.psum_scatter(matrices[1], 'batch', scatter_dimension=0, tiled=True)  31.4 us
    unnamed x91, local copies, waits for them, and re-layouts  25.9 us
  transfers between devices with their start and end apart: 10, of which 8 were waited for; matrix products, arithmetic and copies ran while one was open for 13% of the time, Pallas kernels for 0%

commit v1 on v0

v1 whole, which is shorter than its diff:
```python
import functools

import jax
import jax.numpy as jnp
from jax import lax
from jax.experimental import pallas as pl
from jax.experimental.pallas import tpu as pltpu
from jax.sharding import PartitionSpec as P

H = 12
BF = jnp.bfloat16
F32 = jnp.float32
MESH = pl.DeviceIdType.MESH
V_BQ, V_BV, V_BO, V_G1, V_S1, V_BOUT, V_G2, V_S2, V_CP, V_BIN = range(10)


def nn(a, b):
    return lax.dot_general(a, b, (((1,), (0,)), ((), ())), preferred_element_type=F32)


def nt(a, b):
    return lax.dot_general(a, b, (((1,), (1,)), ((), ())), preferred_element_type=F32)


def tn(a, b):
    return lax.dot_general(a, b, (((0,), (0,)), ((), ())), preferred_element_type=F32)


def aligned(index, size):
    return pl.ds(pl.multiple_of(index * size, size), size)


def norm_back(grad, normed, inv_std):
    first = jnp.mean(grad, 0, keepdims=True)
    second = jnp.mean(grad * normed, 0, keepdims=True)
    return inv_std * (grad - first - normed * second)


def layer_kernel(dims, *refs):
    seq_count, block_len, width, ff = dims
    (
        hidden_ref,
        cot_ref,
        len_ref,
        vec_ref,
        w_qkv_hbm,
        w_o_hbm,
        w_in_hbm,
        w_out_hbm,
        out_ref,
        gin_ref,
        pooled_ref,
        vecs_ref,
        gq_ref,
        go_ref,
        gi_ref,
        gt_ref,
        w_qkv,
        w_o,
        w_in,
        w_out,
        x_rows,
        cot_rows,
        x_t,
        qkv_t,
        expo,
        inv_sum,
        att_t,
        normed_one,
        middle_low,
        act,
        slope,
        normed_two,
        grad_second,
        grad_first,
        low_a,
        grad_att,
        grad_proj,
        rows_out,
        rows_gin,
        stage,
        vec_t,
        vec_cols,
        w_sem,
        out_sem,
        x_send,
        x_recv,
        c_send,
        c_recv,
        o_send,
        o_recv,
        g_send,
        g_recv,
        own_sem,
    ) = refs
    seq_len = seq_count * block_len
    head = width // H
    me_b = lax.axis_index("batch")
    me_s = lax.axis_index("seq")

    loads = []
    for k, (src, dst) in enumerate(
        ((w_qkv_hbm, w_qkv), (w_o_hbm, w_o), (w_in_hbm, w_in), (w_out_hbm, w_out))
    ):
        load = pltpu.make_async_copy(src, dst, w_sem.at[k])
        load.start()
        loads.append(load)

    barrier = pltpu.get_barrier_semaphore()
    for d in range(1, seq_count):
        pl.semaphore_signal(
            barrier,
            inc=1,
            device_id=(me_b, lax.rem(me_s + d, seq_count)),
            device_id_type=MESH,
        )
    pl.semaphore_wait(barrier, seq_count - 1)

    def exchange(src, dst, own, send_sem, recv_sem):
        copies = []
        for d in range(1, seq_count):
            to = lax.rem(me_s + d, seq_count)
            copy = pltpu.make_async_remote_copy(
                src_ref=src.at[to],
                dst_ref=dst.at[me_s],
                send_sem=send_sem.at[d],
                recv_sem=recv_sem.at[d],
                device_id=(me_b, to),
                device_id_type=MESH,
            )
            copy.start()
            copies.append(copy)
        copy = pltpu.make_async_copy(src.at[me_s], dst.at[me_s], own_sem.at[own])
        copy.start()
        copies.append(copy)
        return copies

    def finish(copies):
        for copy in copies:
            copy.wait()

    hidden_copies = exchange(hidden_ref, x_rows, 0, x_send, x_recv)

    vec_cols[...] = jnp.zeros((width, 128), F32)
    vec_t[...] = jnp.transpose(vec_ref[...].astype(F32))

    def column(index):
        return vec_t[:, index : index + 1]

    length = len_ref[0]
    inv_len = 1.0 / jnp.full((1, seq_len), length, jnp.int32).astype(F32)
    token_at = lax.broadcasted_iota(jnp.int32, (1, seq_len), 1)
    live = jnp.where(token_at < length, 1.0, 0.0).astype(F32)
    key_at = lax.broadcasted_iota(jnp.int32, (seq_len, 1), 0)
    key_bias = jnp.where(key_at < length, 0.0, -1e30).astype(F32)

    finish(hidden_copies)
    cot_copies = exchange(cot_ref, cot_rows, 1, c_send, c_recv)
    x_t[...] = jnp.transpose(x_rows[...].reshape(seq_len, width))

    loads[0].wait()
    scale = head ** (-0.5)
    qkv_t[0:width, :] = (
        (tn(w_qkv[:, 0:width], x_t[...]) + column(V_BQ)) * scale
    ).astype(BF)
    qkv_t[width : 2 * width, :] = tn(w_qkv[:, width : 2 * width], x_t[...]).astype(BF)
    qkv_t[2 * width :, :] = (tn(w_qkv[:, 2 * width :], x_t[...]) + column(V_BV)).astype(BF)

    def head_rows(h, third):
        return pl.ds(pl.multiple_of(h * head + third * width, head), head)

    def attend(h, carry):
        scores = tn(qkv_t[head_rows(h, 1), :], qkv_t[head_rows(h, 0), :]) + key_bias
        top = jnp.max(scores, 0, keepdims=True)
        weights = jnp.exp(scores - top)
        inverse = 1.0 / jnp.sum(weights, 0, keepdims=True)
        weights_low = weights.astype(BF)
        expo[aligned(h, seq_len), :] = weights_low
        inv_sum[aligned(h, 8), :] = jnp.broadcast_to(inverse, (8, seq_len))
        att_t[head_rows(h, 0), :] = (nn(qkv_t[head_rows(h, 2), :], weights_low) * inverse).astype(BF)
        return carry

    lax.fori_loop(0, H, attend, 0)

    loads[1].wait()
    summed = x_t[...].astype(F32) + (tn(w_o[...], att_t[...]) + column(V_BO))
    centred = summed - jnp.mean(summed, 0, keepdims=True)
    inv_one = lax.rsqrt(jnp.mean(centred * centred, 0, keepdims=True) + 1e-12)
    normed_one[...] = centred * inv_one
    middle_low[...] = (normed_one[...] * column(V_G1) + column(V_S1)).astype(BF)

    loads[2].wait()
    parts = ff // width
    for i in range(parts):
        rows = slice(i * width, (i + 1) * width)
        pre = tn(w_in[:, rows], middle_low[...]) + column(V_BIN + i)
        cumulative = 0.5 * (1.0 + lax.erf(pre * 0.7071067811865476))
        density = jnp.exp(-0.5 * pre * pre) * 0.3989422804014327
        act[rows, :] = (pre * cumulative).astype(BF)
        slope[rows, :] = (cumulative + pre * density).astype(BF)
    loads[3].wait()
    middle = normed_one[...] * column(V_G1) + column(V_S1)
    summed = middle + (tn(w_out[...], act[...]) + column(V_BOUT))
    centred = summed - jnp.mean(summed, 0, keepdims=True)
    inv_two = lax.rsqrt(jnp.mean(centred * centred, 0, keepdims=True) + 1e-12)
    normed_two[...] = centred * inv_two
    output = normed_two[...] * column(V_G2) + column(V_S2)
    pooled_col = jnp.sum(output * (live * inv_len), 1, keepdims=True)
    rows_out[...] = jnp.transpose(output.astype(BF)).reshape(seq_count, block_len, width)
    out_copies = exchange(rows_out, out_ref, 2, o_send, o_recv)

    finish(cot_copies)
    grad_final = jnp.transpose(cot_rows[...].reshape(seq_len, width)).astype(F32)
    grad_final = grad_final + column(V_CP) * (live * inv_len)
    vec_cols[:, 0:1] = jnp.sum(grad_final * normed_two[...], 1, keepdims=True)
    vec_cols[:, 1:2] = jnp.sum(grad_final, 1, keepdims=True)
    grad_second[...] = norm_back(grad_final * column(V_G2), normed_two[...], inv_two)
    low_a[...] = grad_second[...].astype(BF)
    vec_cols[:, 2:3] = jnp.sum(low_a[...].astype(F32), 1, keepdims=True)

    def put(value, dst, sem):
        rows, columns = value.shape
        stage[0:rows, 0:columns] = value.astype(BF)
        copy = pltpu.make_async_copy(stage.at[0:rows, 0:columns], dst, out_sem.at[sem])
        copy.start()
        copy.wait()

    for i in range(parts):
        rows = slice(i * width, (i + 1) * width)
        put(nt(act[rows, :], low_a[...]), gt_ref.at[rows, :], 0)

    for i in range(parts):
        rows = slice(i * width, (i + 1) * width)
        grad_act = nn(w_out[rows, :], low_a[...]).astype(BF)
        grad_pre = (grad_act.astype(F32) * slope[rows, :].astype(F32)).astype(BF)
        slope[rows, :] = grad_pre
        vec_cols[:, 3 + i : 4 + i] = jnp.sum(grad_pre.astype(F32), 1, keepdims=True)
    put(nt(middle_low[...], slope[...]), gi_ref, 0)
    grad_middle = grad_second[...] + nn(w_in[...], slope[...])

    vec_cols[:, 7:8] = jnp.sum(grad_middle * normed_one[...], 1, keepdims=True)
    vec_cols[:, 8:9] = jnp.sum(grad_middle, 1, keepdims=True)
    grad_first[...] = norm_back(grad_middle * column(V_G1), normed_one[...], inv_one)
    low_a[...] = grad_first[...].astype(BF)
    vec_cols[:, 9:10] = jnp.sum(low_a[...].astype(F32), 1, keepdims=True)
    put(nt(att_t[...], low_a[...]), go_ref, 0)
    grad_heads = nn(w_o[...], low_a[...])
    for h in range(H):
        rows = slice(h * head, (h + 1) * head)
        grad_att[rows, :] = (grad_heads[rows, :] * inv_sum[h * 8 : h * 8 + 1, :]).astype(BF)

    def attend_back(h, carry):
        grad = grad_att[head_rows(h, 0), :]
        inner = jnp.sum(grad.astype(F32) * att_t[head_rows(h, 0), :].astype(F32), 0, keepdims=True)
        weights_low = expo[aligned(h, seq_len), :]
        grad_probs = tn(qkv_t[head_rows(h, 2), :], grad)
        grad_scores = (weights_low.astype(F32) * (grad_probs - inner)).astype(BF)
        grad_proj[head_rows(h, 0), :] = (nn(qkv_t[head_rows(h, 1), :], grad_scores) * scale).astype(BF)
        grad_proj[head_rows(h, 1), :] = nt(qkv_t[head_rows(h, 0), :], grad_scores).astype(BF)
        grad_proj[head_rows(h, 2), :] = nt(grad, weights_low).astype(BF)
        return carry

    lax.fori_loop(0, H, attend_back, 0)
    vec_cols[:, 10:11] = jnp.sum(grad_proj[0:width, :].astype(F32), 1, keepdims=True)
    vec_cols[:, 11:12] = jnp.sum(grad_proj[2 * width :, :].astype(F32), 1, keepdims=True)
    vec_cols[:, 12:13] = pooled_col
    grad_in = nn(w_qkv[...], grad_proj[...]) + grad_first[...]
    rows_gin[...] = jnp.transpose(grad_in.astype(BF)).reshape(seq_count, block_len, width)
    gin_copies = exchange(rows_gin, gin_ref, 3, g_send, g_recv)
    put(nt(x_t[...], grad_proj[...]), gq_ref, 0)
    vecs_ref[...] = jnp.transpose(vec_cols[...])[0:16, :]
    pooled_ref[...] = jnp.transpose(vec_cols[...])[8:16, :]
    finish(out_copies)
    finish(gin_copies)


def body(
    hidden_in,
    lengths,
    w_qkv,
    b_q,
    b_v,
    w_o,
    b_o,
    gain_one,
    shift_one,
    w_in,
    b_in,
    w_out,
    b_out,
    gain_two,
    shift_two,
    cot_hidden,
    cot_pooled,
):
    seq_count = lax.axis_size("seq")
    seqs_here, block_len, width = hidden_in.shape
    ff = w_in.shape[1]
    seq_len = seq_count * block_len
    assert seqs_here == seq_count
    me_s = lax.axis_index("seq")
    own_length = lax.dynamic_slice(lengths, (me_s,), (1,))
    own_cot = lax.dynamic_slice(cot_pooled, (me_s, 0), (1, width)).reshape(width)
    vectors = (b_q, b_v, b_o, gain_one, shift_one, b_out, gain_two, shift_two, own_cot, b_in)
    vec = jnp.concatenate(vectors).reshape(-1, width)
    vec = jnp.pad(vec, ((0, 128 - vec.shape[0]), (0, 0)))

    anywhere = pl.BlockSpec(memory_space=pl.ANY)
    vmem = pl.BlockSpec(memory_space=pltpu.VMEM)
    smem = pl.BlockSpec(memory_space=pltpu.SMEM)
    rows = jax.ShapeDtypeStruct(hidden_in.shape, BF)
    outs = pl.pallas_call(
        functools.partial(layer_kernel, (seq_count, block_len, width, ff)),
        out_shape=(
            rows,
            rows,
            jax.ShapeDtypeStruct((8, width), F32),
            jax.ShapeDtypeStruct((16, width), F32),
            jax.ShapeDtypeStruct(w_qkv.shape, BF),
            jax.ShapeDtypeStruct(w_o.shape, BF),
            jax.ShapeDtypeStruct(w_in.shape, BF),
            jax.ShapeDtypeStruct(w_out.shape, BF),
        ),
        in_specs=[anywhere, anywhere, smem, vmem, anywhere, anywhere, anywhere, anywhere],
        out_specs=(anywhere, anywhere, vmem, vmem, anywhere, anywhere, anywhere, anywhere),
        scratch_shapes=[
            pltpu.VMEM(w_qkv.shape, BF),
            pltpu.VMEM(w_o.shape, BF),
            pltpu.VMEM(w_in.shape, BF),
            pltpu.VMEM(w_out.shape, BF),
            pltpu.VMEM((seq_count, block_len, width), BF),
            pltpu.VMEM((seq_count, block_len, width), BF),
            pltpu.VMEM((width, seq_len), BF),
            pltpu.VMEM((3 * width, seq_len), BF),
            pltpu.VMEM((H * seq_len, seq_len), BF),
            pltpu.VMEM((H * 8, seq_len), F32),
            pltpu.VMEM((width, seq_len), BF),
            pltpu.VMEM((width, seq_len), F32),
            pltpu.VMEM((width, seq_len), BF),
            pltpu.VMEM((ff, seq_len), BF),
            pltpu.VMEM((ff, seq_len), BF),
            pltpu.VMEM((width, seq_len), F32),
            pltpu.VMEM((width, seq_len), F32),
            pltpu.VMEM((width, seq_len), F32),
            pltpu.VMEM((width, seq_len), BF),
            pltpu.VMEM((width, seq_len), BF),
            pltpu.VMEM((3 * width, seq_len), BF),
            pltpu.VMEM((seq_count, block_len, width), BF),
            pltpu.VMEM((seq_count, block_len, width), BF),
            pltpu.VMEM((width, ff), BF),
            pltpu.VMEM((width, 128), F32),
            pltpu.VMEM((width, 128), F32),
            pltpu.SemaphoreType.DMA((4,)),
            pltpu.SemaphoreType.DMA((1,)),
        ]
        + [pltpu.SemaphoreType.DMA((seq_count,))] * 8
        + [pltpu.SemaphoreType.DMA((4,))],
        compiler_params=pltpu.CompilerParams(
            collective_id=0, has_side_effects=True, vmem_limit_bytes=60 * 2**20
        ),
        name="encoder_layer",
    )(hidden_in, cot_hidden, own_length, vec, w_qkv, w_o, w_in, w_out)
    out_hidden, grad_in, pooled_row, vecs, g_qkv, g_o, g_in, g_out = outs
    pooled = lax.all_gather(pooled_row[4], "seq", axis=0)

    def scatter(grad):
        part = lax.psum_scatter(grad.astype(F32), "batch", scatter_dimension=0, tiled=True)
        return lax.psum_scatter(
            part.astype(BF), "seq", scatter_dimension=1, tiled=True
        ).astype(F32)

    total = lax.psum(vecs[:12], ("batch", "seq"))
    return (
        out_hidden,
        pooled,
        grad_in,
        scatter(g_qkv),
        total[10],
        total[11],
        scatter(g_o),
        total[9],
        total[7],
        total[8],
        scatter(g_in),
        total[3:7].reshape(ff),
        scatter(g_out),
        total[2],
        total[0],
        total[1],
    )


def solution(mesh):
    rows = P("batch", "seq", None)
    shard = P("batch", "seq")
    in_specs = (rows, P("batch")) + (P(),) * 13 + (rows, P("batch", None))
    out_specs = (
        rows,
        P("batch", None),
        rows,
        shard,
        P(),
        P(),
        shard,
        P(),
        P(),
        P(),
        shard,
        P(),
        shard,
        P(),
        P(),
        P(),
    )
    return jax.shard_map(body, mesh=mesh, in_specs=in_specs, out_specs=out_specs, check_vma=False)
```

time: 750 us -> 423 us (0.56)
  waiting for transfers between devices: 438 us -> 233 us
  matrix products: 120 us -> 0 us
  Pallas kernels: 0 us -> 94.3 us
  local copies, waits for them, and re-layouts: 68.6 us -> 24.6 us
  other arithmetic: 42.8 us -> 3.01 us
    dot_general x17 -> x0, matrix products: 109 us -> none  [the longest x1 19.1 us: ffn_front(): jnp.dot(middle_low, w_in, preferred_element_type=jnp.float32)]
    all_gather x1 -> x0, waiting for transfers between devices: 101 us -> none  [run_layer(): whole_kv = lax.all_gather(local_kv, 'seq', axis=1, tiled=True)]
    pallas_call x0 -> x1, Pallas kernels: none -> 94.3 us  [body(): pl.pallas_call(functools.partial(layer_kernel, (seq_count, block_len, wid...]
    unnamed x13 -> x11, waiting for transfers between devices: 65.2 us -> 11.4 us
    reduce_scatter x6 -> x5, waiting for transfers between devices: 272 us -> 221 us  [the longest x4 200 us: scatter(): lax.psum_scatter(grad.astype(F32), 'batch', scatter_dimension=0, tiled=True)]
    convert_element_type x17 -> x3, other arithmetic: 24.6 us -> 3.01 us  [scatter(): return lax.psum_scatter(part.astype(BF), 'seq', scatter_dimension=1, tile...]
    slice x6 -> x2, local copies, waits for them, and re-layouts: 21.1 us -> 0.66 us  [the longest x1 0.66 us: body(): total[1]]
    psum x2 -> x1, blocking collectives: 59.8 us -> 39.7 us  [body(): total = lax.psum(vecs[:12], ('batch', 'seq'))]
  transfers between devices with their start and end apart: 10 -> 8, of which waited for: 8 -> 6; matrix products, arithmetic and copies ran while one was open for 13% -> 3% of each run, Pallas kernels for 0% -> 0%
where the time goes in v1:
time: 423 us; the launch traced here: 422 us
  waiting for transfers between devices  233 us (55%)
  Pallas kernels  94.3 us (22%)
  blocking collectives  52.8 us (12%)
  local copies, waits for them, and re-layouts  24.6 us (6%)
  between operations  14.3 us (3%)
    reduce_scatter x4, waiting for transfers between devices, scatter(): lax.psum_scatter(grad.astype(F32), 'batch', scatter_dimension=0, tiled=True)  200 us
    pallas_call x1, Pallas kernels, body(): pl.pallas_call(functools.partial(layer_kernel, (seq_count, block_len, wid...  94.3 us
    psum x1, blocking collectives, body(): total = lax.psum(vecs[:12], ('batch', 'seq'))  39.7 us
    reduce_scatter x1, waiting for transfers between devices, scatter(): lax.psum_scatter(part.astype(BF), 'seq', scatter_dimension=1, tiled=True)  21 us
    unnamed x28, local copies, waits for them, and re-layouts  20.5 us
    all_gather x1, blocking collectives, body(): pooled = lax.all_gather(pooled_row[4], 'seq', axis=0)  13.1 us
    unnamed x11, waiting for transfers between devices  11.4 us
  transfers between devices with their start and end apart: 8, of which 6 were waited for; matrix products, arithmetic and copies ran while one was open for 3% of the time, Pallas kernels for 0%

profile of v1, /device:TPU:0, one launch (start us, length us, event | category | flops | bytes accessed | tf_op | source)
XLA Modules:
  0.0 421.8 jit_solution(11665580187543885625)
XLA Ops:
  7.9 0.9 dynamic-update-slice
  8.8 0.8 dynamic-update-slice.1
  9.6 0.9 dynamic-update-slice.2
  10.5 0.9 dynamic-update-slice.3
  11.3 0.9 dynamic-update-slice.4
  12.2 0.8 dynamic-update-slice.5
  13.0 0.9 dynamic-update-slice.6
  13.9 0.9 dynamic-update-slice.7
  14.9 0.9 dynamic-update-slice.9
  15.8 1.2 dynamic_slice.6.refs_2_
  17.8 94.3 %encoder_layer.1 = (bf16[4,128,768]{2,1,0:T(8,128)(2,1)}, bf16[4,128,768]{2,1,0:T(8,128)(2,1)}, f32[8,768]{1,0:T(8,128)}, f32[16,768]{1,0:T(8,128)}, bf16[768,23...) custom-call(bf16[4,128,768]{2,1,0:T(8,128)(2,1)} %refs_0_.1, ...), custom_call_target="tpu_custom_call" | custom-call | tf_op jit(solution)/shard_map/encoder_layer/pallas_call | solution.py:312
  112.2 0.7 reduce-scatter.15.cloned.1.call-update
  114.3 39.2 %reduce-scatter.17.cloned.1.call-done = bf16[96,768]{1,0:T(8,128)(2,1)} async-done(((bf16[768,768]{1,0:T(8,128)(2,1)}), bf16[96,768]{1,0:T(8,128)(2,1)}) %reduce-scatter.17.cloned.1.call-update) | async-done | bytes 147472 | tf_op jit(solution)/shard_map/reduce_scatter | solution.py:367
  153.5 1.7 copy.37
  155.3 50.2 %reduce-scatter.15.cloned.1.call-done = bf16[96,2304]{1,0:T(8,128)(2,1)} async-done(((bf16[768,2304]{1,0:T(8,128)(2,1)}), bf16[96,2304]{1,0:T(8,128)(2,1)}) %reduce-scatter.15.cloned.1.call-update) | async-done | bytes 442384 | tf_op jit(solution)/shard_map/reduce_scatter | solution.py:367
  205.5 2.1 copy.35
  207.6 55.6 %reduce-scatter.23.cloned.1.call-done = bf16[384,768]{1,0:T(8,128)(2,1)} async-done(((bf16[3072,768]{1,0:T(8,128)(2,1)}), bf16[384,768]{1,0:T(8,128)(2,1)}) %reduce-scatter.23.cloned.1.call-update) | async-done | bytes 589840 | tf_op jit(solution)/shard_map/reduce_scatter | solution.py:367
  263.3 2.1 copy.39
  265.5 55.0 %reduce-scatter.19.cloned.1.call-done = bf16[96,3072]{1,0:T(8,128)(2,1)} async-done(((bf16[768,3072]{1,0:T(8,128)(2,1)}), bf16[96,3072]{1,0:T(8,128)(2,1)}) %reduce-scatter.19.cloned.1.call-update) | async-done | bytes 589840 | tf_op jit(solution)/shard_map/reduce_scatter | solution.py:367
  320.5 39.7 %psum.7 = f32[12,768]{1,0:T(8,128)S(1)} all-reduce(f32[12,768]{1,0:T(8,128)S(1)} %bitcast.17), channel_id=1, replica_groups=mesh['batch'=8,'seq'=4] {'batch','seq'}, use_global_device_ids=true, to_apply=%region_2.3 | all-reduce | flops 9216 | bytes 73728 | tf_op jit(solution)/shard_map/psum | solution.py:372
  360.9 0.7 slice_bitcast_fusion
  361.6 13.1 %all-gather = f32[4,1,768]{2,1,0:T(1,128)S(1)} all-gather(f32[1,1,768]{2,1,0:T(1,128)S(1)} %slice_bitcast_fusion), channel_id=1, replica_groups=mesh['batch'=8,'seq'=4] {'seq'}, dimensions={0}, use_global_device_ids=true | all-gather | bytes 15360 | tf_op jit(solution)/shard_map/all_gather | solution.py:364
  376.0 0.9 copy.38
  377.5 1.0 copy.36
  378.6 0.7 convert_element_type.40
  379.3 9.4 %reduce-scatter.29.cloned.1.call-done = bf16[192,384]{1,0:T(8,128)(2,1)} async-done(((bf16[768,384]{1,0:T(8,128)(2,1)}), bf16[192,384]{1,0:T(8,128)(2,1)}) %reduce-scatter.29.cloned.1.call-update) | async-done | bytes 147472
  388.7 1.0 copy.40
  389.8 0.8 copy.34
  390.6 21.0 %reduce-scatter.21.cloned.1.call-done = bf16[96,768]{1,0:T(8,128)(2,1)} async-done(((bf16[96,3072]{1,0:T(8,128)(2,1)}), bf16[96,768]{1,0:T(8,128)(2,1)}) %reduce-scatter.21.cloned.1.call-update) | async-done | bytes 147472 | tf_op jit(solution)/shard_map/reduce_scatter | solution.py:368
  411.6 1.6 convert_element_type.46
  413.2 0.9 copy.56
  414.1 0.9 copy.57
  (35 shorter events, 5.7 us)
Async XLA Ops:
  7.2 0.7 copy-start
  7.2 146.3 %reduce-scatter.17.cloned.1.call-start = ((), (), s32[]{:S(2)}) async-start(), calls=%async_computation.9 | async-start | bytes 1327104 | tf_op jit(solution)/shard_map/reduce_scatter | solution.py:367
  112.1 93.4 %reduce-scatter.15.cloned.1.call-start = ((), (), s32[]{:S(2)}) async-start(), calls=%async_computation.8 | async-start | bytes 3981312 | tf_op jit(solution)/shard_map/reduce_scatter | solution.py:367
  112.9 150.4 %reduce-scatter.23.cloned.1.call-start = ((), (), s32[]{:S(2)}) async-start(), calls=%async_computation.12 | async-start | bytes 5308416 | tf_op jit(solution)/shard_map/reduce_scatter | solution.py:367
  113.6 206.9 %copy-start.3 = (f32[16,768]{1,0:T(8,128)S(1)}, f32[16,768]{1,0:T(8,128)}, u32[]{:S(2)}) copy-start(f32[16,768]{1,0:T(8,128)} %get-tuple-element.28) | copy-start | bytes 147460
  113.6 206.9 %reduce-scatter.19.cloned.1.call-start = ((), (), s32[]{:S(2)}) async-start(), calls=%async_computation.10 | async-start | bytes 5308416 | tf_op jit(solution)/shard_map/reduce_scatter | solution.py:367
  113.7 299.6 %copy-start.2 = (bf16[4,128,768]{2,1,0:T(8,128)(2,1)S(1)}, bf16[4,128,768]{2,1,0:T(8,128)(2,1)}, u32[]{:S(2)}) copy-start(bf16[4,128,768]{2,1,0:T(8,128)(2,1)} %get-tuple-element.88) | copy-start | bytes 2359300
  114.2 299.9 %copy-start.1 = (bf16[4,128,768]{2,1,0:T(8,128)(2,1)S(1)}, bf16[4,128,768]{2,1,0:T(8,128)(2,1)}, u32[]{:S(2)}) copy-start(bf16[4,128,768]{2,1,0:T(8,128)(2,1)} %get-tuple-element.90) | copy-start | bytes 2359300
  114.2 261.7 %reduce-scatter.27.cloned.1.call-start = ((), (), s32[]{:S(2)}) async-start(), calls=%async_computation.14 | async-start | bytes 245760
  155.3 222.2 %reduce-scatter.25.cloned.1.call-start = ((), (), s32[]{:S(2)}) async-start(), calls=%async_computation.13 | async-start | bytes 737280
  207.6 181.1 %reduce-scatter.29.cloned.1.call-start = ((), (), s32[]{:S(2)}) async-start(), calls=%async_computation.15 | async-start | bytes 737280
  265.4 146.2 %reduce-scatter.21.cloned.1.call-start = ((), (), s32[]{:S(2)}) async-start(), calls=%async_computation.11 | async-start | bytes 737280 | tf_op jit(solution)/shard_map/reduce_scatter | solution.py:368
Sparse Core Ops, SparseCore 0:
  112.2 41.2 reduce-scatter.16
  157.4 48.0 reduce-scatter.14
  209.3 53.8 reduce-scatter.22
  266.6 53.8 reduce-scatter.18
  323.3 19.3 reduce-scatter.26
  345.3 20.3 reduce-scatter.24
  368.6 20.0 reduce-scatter.28
  391.0 20.5 reduce-scatter.20

commit v2 on v1

v2 whole, which is shorter than its diff:
```python
import functools

import jax
import jax.numpy as jnp
from jax import lax
from jax.experimental import pallas as pl
from jax.experimental.pallas import tpu as pltpu
from jax.sharding import PartitionSpec as P

H = 12
BF = jnp.bfloat16
F32 = jnp.float32
MESH = pl.DeviceIdType.MESH
V_BQ, V_BV, V_BO, V_G1, V_S1, V_BOUT, V_G2, V_S2, V_CP, V_BIN = range(10)


def nn(a, b):
    return lax.dot_general(a, b, (((1,), (0,)), ((), ())), preferred_element_type=F32)


def nt(a, b):
    return lax.dot_general(a, b, (((1,), (1,)), ((), ())), preferred_element_type=F32)


def tn(a, b):
    return lax.dot_general(a, b, (((0,), (0,)), ((), ())), preferred_element_type=F32)


def aligned(index, size):
    return pl.ds(pl.multiple_of(index * size, size), size)


def norm_back(grad, normed, inv_std):
    first = jnp.mean(grad, 0, keepdims=True)
    second = jnp.mean(grad * normed, 0, keepdims=True)
    return inv_std * (grad - first - normed * second)


def add_low(a, b):
    return (a.astype(F32) + b.astype(F32)).astype(BF)


G_OUT, G_IN, G_O, G_QKV = range(4)


def layer_kernel(dims, *refs):
    batch_count, seq_count, block_len, width, ff, fused = dims
    refs = list(refs)

    def take(count):
        taken = refs[:count]
        del refs[:count]
        return taken

    hidden_ref, cot_ref, len_ref, cot_pool_ref = take(4)
    vectors = take(9)
    w_qkv_hbm, w_o_hbm, w_in_hbm, w_out_hbm = take(4)
    out_ref, gin_ref, pooled_ref, vecs_ref = take(4)
    grad_refs = take(4)
    w_qkv, w_o, w_in, w_out = take(4)
    x_rows, cot_rows, x_t, qkv_t, expo, inv_sum, att_t = take(7)
    normed_one, middle_low, act, slope, normed_two, grad_second, low_a, grad_att = take(8)
    vec_cols, w_sem, own_sem = take(3)
    x_send, x_recv, c_send, c_recv, o_send, o_recv, g_send, g_recv = take(8)
    if fused:
        send_core = take(3)
        held_core, held_one, held_two, held_z, z_one, z_two = (take(4) for _ in range(6))
        core_send, core_recv, link_send, link_recv = take(4)
        vec_own, vec_in, pool_own, pool_in, v_send, v_recv, p_send, p_recv = take(8)
    else:
        stage, put_sem = take(2)
    seq_len = seq_count * block_len
    head = width // H
    parts = ff // width
    me_b = lax.axis_index("batch")
    me_s = lax.axis_index("seq")

    loads = []
    for k, (src, dst) in enumerate(
        ((w_qkv_hbm, w_qkv), (w_o_hbm, w_o), (w_in_hbm, w_in), (w_out_hbm, w_out))
    ):
        load = pltpu.make_async_copy(src, dst, w_sem.at[k])
        load.start()
        loads.append(load)

    def flipped(index, bit):
        return index + bit - 2 * bit * lax.rem(index // bit, 2)

    def seq_peer(d):
        return (me_b, lax.rem(me_s + d, seq_count))

    core, at_x, at_y = lax.rem(me_b, 2), lax.rem(me_b // 2, 2), lax.rem(me_b // 4, 2)
    z_lo, z_hi = lax.rem(me_s, 2), lax.rem(me_s // 2, 2)
    to_core, to_x, to_y = ((flipped(me_b, bit), me_s) for bit in (1, 2, 4))
    to_z_lo, to_z_hi = ((me_b, flipped(me_s, bit)) for bit in (1, 2))

    barrier = pltpu.get_barrier_semaphore()
    greeted = [seq_peer(d) for d in range(1, seq_count)]
    if fused:
        greeted += [to_core, to_x, to_y]
    for device in greeted:
        pl.semaphore_signal(barrier, inc=1, device_id=device, device_id_type=MESH)
    pl.semaphore_wait(barrier, len(greeted))

    def remote(src, dst, device, send_sem, recv_sem):
        copy = pltpu.make_async_remote_copy(
            src_ref=src,
            dst_ref=dst,
            send_sem=send_sem,
            recv_sem=recv_sem,
            device_id=device,
            device_id_type=MESH,
        )
        copy.start()
        return copy

    def exchange(src, dst, own, send_sem, recv_sem):
        copies = []
        for d in range(1, seq_count):
            to = lax.rem(me_s + d, seq_count)
            copies.append(
                remote(src.at[to], dst.at[me_s], seq_peer(d), send_sem.at[d], recv_sem.at[d])
            )
        copy = pltpu.make_async_copy(src.at[me_s], dst.at[me_s], own_sem.at[own])
        copy.start()
        copies.append(copy)
        return copies

    def finish(copies):
        for copy in copies:
            copy.wait()

    hidden_copies = exchange(hidden_ref, x_rows, 0, x_send, x_recv)

    cot_pool = cot_pool_ref[...].astype(F32)
    is_mine = lax.broadcasted_iota(jnp.int32, cot_pool.shape, 0) == me_s
    cot_pool = jnp.sum(jnp.where(is_mine, cot_pool, 0.0), 0, keepdims=True)
    rows = [ref[...].astype(F32).reshape(1, width) for ref in vectors[:8]] + [cot_pool]
    for i in range(parts):
        rows.append(vectors[8][i * width : (i + 1) * width].astype(F32).reshape(1, width))
    rows.append(jnp.zeros((128 - len(rows), width), F32))
    vec_t = jnp.transpose(jnp.concatenate(rows, 0))
    vec_cols[...] = jnp.zeros((width, 128), F32)

    def column(index):
        return vec_t[:, index : index + 1]

    length = len_ref[me_s]
    inv_len = 1.0 / jnp.full((1, seq_len), length, jnp.int32).astype(F32)
    token_at = lax.broadcasted_iota(jnp.int32, (1, seq_len), 1)
    live = jnp.where(token_at < length, 1.0, 0.0).astype(F32)
    key_at = lax.broadcasted_iota(jnp.int32, (seq_len, 1), 0)
    key_bias = jnp.where(key_at < length, 0.0, -1e30).astype(F32)

    finish(hidden_copies)
    cot_copies = exchange(cot_ref, cot_rows, 1, c_send, c_recv)
    x_t[...] = jnp.transpose(x_rows[...].reshape(seq_len, width))

    loads[0].wait()
    scale = head ** (-0.5)
    qkv_t[0:width, :] = (
        (tn(w_qkv[:, 0:width], x_t[...]) + column(V_BQ)) * scale
    ).astype(BF)
    qkv_t[width : 2 * width, :] = tn(w_qkv[:, width : 2 * width], x_t[...]).astype(BF)
    qkv_t[2 * width :, :] = (tn(w_qkv[:, 2 * width :], x_t[...]) + column(V_BV)).astype(BF)

    def head_rows(h, third):
        return pl.ds(pl.multiple_of(h * head + third * width, head), head)

    def attend(h, carry):
        scores = tn(qkv_t[head_rows(h, 1), :], qkv_t[head_rows(h, 0), :]) + key_bias
        top = jnp.max(scores, 0, keepdims=True)
        weights = jnp.exp(scores - top)
        inverse = 1.0 / jnp.sum(weights, 0, keepdims=True)
        weights_low = weights.astype(BF)
        expo[aligned(h, seq_len), :] = weights_low
        inv_sum[aligned(h, 8), :] = jnp.broadcast_to(inverse, (8, seq_len))
        att_t[head_rows(h, 0), :] = (nn(qkv_t[head_rows(h, 2), :], weights_low) * inverse).astype(BF)
        return carry

    lax.fori_loop(0, H, attend, 0)

    loads[1].wait()
    summed = x_t[...].astype(F32) + (tn(w_o[...], att_t[...]) + column(V_BO))
    centred = summed - jnp.mean(summed, 0, keepdims=True)
    inv_one = lax.rsqrt(jnp.mean(centred * centred, 0, keepdims=True) + 1e-12)
    normed_one[...] = centred * inv_one
    middle_low[...] = (normed_one[...] * column(V_G1) + column(V_S1)).astype(BF)

    loads[2].wait()
    for i in range(parts):
        rows = slice(i * width, (i + 1) * width)
        pre = tn(w_in[:, rows], middle_low[...]) + column(V_BIN + i)
        cumulative = 0.5 * (1.0 + lax.erf(pre * 0.7071067811865476))
        density = jnp.exp(-0.5 * pre * pre) * 0.3989422804014327
        act[rows, :] = (pre * cumulative).astype(BF)
        slope[rows, :] = (cumulative + pre * density).astype(BF)
    loads[3].wait()
    middle = normed_one[...] * column(V_G1) + column(V_S1)
    summed = middle + (tn(w_out[...], act[...]) + column(V_BOUT))
    centred = summed - jnp.mean(summed, 0, keepdims=True)
    inv_two = lax.rsqrt(jnp.mean(centred * centred, 0, keepdims=True) + 1e-12)
    normed_two[...] = centred * inv_two
    output = normed_two[...] * column(V_G2) + column(V_S2)
    pooled_col = jnp.sum(output * (live * inv_len), 1, keepdims=True)
    rows_out = x_rows
    rows_out[...] = jnp.transpose(output.astype(BF)).reshape(seq_count, block_len, width)
    out_copies = exchange(rows_out, out_ref, 2, o_send, o_recv)

    finish(cot_copies)
    grad_final = jnp.transpose(cot_rows[...].reshape(seq_len, width)).astype(F32)
    grad_final = grad_final + column(V_CP) * (live * inv_len)
    vec_cols[:, 0:1] = jnp.sum(grad_final * normed_two[...], 1, keepdims=True)
    vec_cols[:, 1:2] = jnp.sum(grad_final, 1, keepdims=True)
    grad_second[...] = norm_back(grad_final * column(V_G2), normed_two[...], inv_two)
    low_a[...] = grad_second[...].astype(BF)
    vec_cols[:, 2:3] = jnp.sum(low_a[...].astype(F32), 1, keepdims=True)

    def whole_grad(m):
        if m == G_OUT:
            rows, columns = act, low_a
        elif m == G_IN:
            rows, columns = middle_low, slope
        elif m == G_O:
            rows, columns = att_t, low_a
        else:
            rows, columns = x_t, qkv_t
        return rows, columns

    def put(m):
        rows, columns = whole_grad(m)
        for i in range(rows.shape[0] // width):
            value = nt(rows[i * width : (i + 1) * width, :], columns[...])
            here = stage.at[:, 0 : value.shape[1]]
            here[...] = value.astype(BF)
            copy = pltpu.make_async_copy(
                here, grad_refs[m].at[i * width : (i + 1) * width, :], put_sem.at[0]
            )
            copy.start()
            copy.wait()

    flight = {}

    def partial(m, which):
        rows, columns = whole_grad(m)
        deep = rows.shape[0] // batch_count
        picked = [rows[aligned(2 * j + which, deep), :] for j in range(4)]
        value = nt(jnp.concatenate(picked, 0), columns[...])
        half = value.shape[1] // 2
        tile = half // parts if m == G_IN else half
        for j in range(4):
            for h in range(2):
                for t in range(half // tile):
                    start = h * half + t * tile
                    block = value[j * deep : (j + 1) * deep, start : start + tile]
                    yield h, j, slice(t * deep, (t + 1) * deep), block

    def core_buffer(m):
        return send_core[max(m - 1, 0)]

    def to_core_start(m):
        buffer = core_buffer(m)
        if m == G_IN:
            for copy in flight[G_OUT, 0]:
                copy.wait_send()
        for h, j, rows, block in partial(m, 1 - core):
            buffer[h, j // 2, j % 2, rows, :] = block.astype(BF)
        flight[m, 0] = [
            remote(buffer, held_core[m], to_core, core_send.at[m, 0], core_recv.at[m, 0])
        ]

    def to_core_add(m):
        finish(flight[m, 0]) if m != G_OUT else None
        held = held_core[m]
        for h, j, rows, block in partial(m, core):
            held[h, j // 2, j % 2, rows, :] = add_low(held[h, j // 2, j % 2, rows, :], block)
        flight[m, 1] = [
            remote(
                held.at[0, :, 1 - at_x],
                held_one[m].at[0],
                to_x,
                link_send.at[m, 0],
                link_recv.at[m, 0],
            ),
            remote(
                held.at[1, 1 - at_y],
                held_one[m].at[1],
                to_y,
                link_send.at[m, 1],
                link_recv.at[m, 1],
            ),
        ]

    order = ((1 - at_y, 1 - at_x), (at_y, 1 - at_x), (1 - at_y, at_x), (at_y, at_x))

    def first_block(y, x, which):
        deep = ff // batch_count
        row = aligned(4 * y + 2 * x + which, deep)
        return nt(act[row, :], low_a[...])

    def first_start():
        buffer = send_core[0]
        copies = []
        for k, (y, x) in enumerate(order):
            value = first_block(y, x, 1 - core)
            half = value.shape[1] // 2
            buffer[0, y, x] = value[:, :half].astype(BF)
            buffer[1, y, x] = value[:, half:].astype(BF)
            copies.append(
                remote(
                    buffer.at[:, y, x],
                    held_core[G_OUT].at[:, y, x],
                    to_core,
                    core_send.at[G_OUT, k],
                    core_recv.at[G_OUT, k],
                )
            )
        flight[G_OUT, 0] = copies

    def first_add():
        held, after = held_core[G_OUT], held_one[G_OUT]
        copies = []
        for k, (y, x) in enumerate(order):
            flight[G_OUT, 0][k].wait_recv()
            value = first_block(y, x, core)
            half = value.shape[1] // 2
            held[0, y, x] = add_low(held[0, y, x], value[:, :half])
            held[1, y, x] = add_low(held[1, y, x], value[:, half:])
            if k in (0, 1):
                copies.append(
                    remote(
                        held.at[0, y, x],
                        after.at[0, y],
                        to_x,
                        link_send.at[G_OUT, k],
                        link_recv.at[G_OUT, k],
                    )
                )
            if k in (0, 2):
                copies.append(
                    remote(
                        held.at[1, y, x],
                        after.at[1, x],
                        to_y,
                        link_send.at[G_OUT, 2 + k // 2],
                        link_recv.at[G_OUT, 2 + k // 2],
                    )
                )
        flight[G_OUT, 1] = copies

    def second_link(m):
        finish(flight[m, 1])
        held, after = held_core[m], held_one[m]
        after[0, 1 - at_y] = add_low(after[0, 1 - at_y], held[0, 1 - at_y, at_x])
        after[1, 1 - at_x] = add_low(after[1, 1 - at_x], held[1, at_y, 1 - at_x])
        flight[m, 2] = [
            remote(
                after.at[0, 1 - at_y],
                held_two[m].at[0],
                to_y,
                link_send.at[m, 4],
                link_recv.at[m, 4],
            ),
            remote(
                after.at[1, 1 - at_x],
                held_two[m].at[1],
                to_x,
                link_send.at[m, 5],
                link_recv.at[m, 5],
            ),
        ]
        after[0, at_y] = add_low(after[0, at_y], held[0, at_y, at_x])
        after[1, at_x] = add_low(after[1, at_x], held[1, at_y, at_x])

    def first_z(m):
        finish(flight[m, 2])
        after, last, ready = held_one[m], held_two[m], held_z[m]
        for h in range(2):
            mine = after[0, at_y] if h == 0 else after[1, at_x]
            block = add_low(last[h], mine)
            deep, wide = block.shape
            for k in range(2):
                if m == G_IN:
                    ready[h, k] = block[k * (deep // 2) : (k + 1) * (deep // 2), :]
                else:
                    ready[h, k, :, : wide // 2] = block[:, k * (wide // 2) : (k + 1) * (wide // 2)]
        flight[m, 3] = [
            remote(
                ready.at[:, 1 - z_lo], z_one[m], to_z_lo, link_send.at[m, 6], link_recv.at[m, 6]
            )
        ]

    def second_z(m):
        finish(flight[m, 3])
        z_one[m][1 - z_hi] = add_low(z_one[m][1 - z_hi], held_z[m][1 - z_hi, z_lo])
        flight[m, 4] = [
            remote(
                z_one[m].at[1 - z_hi], z_two[m], to_z_hi, link_send.at[m, 7], link_recv.at[m, 7]
            )
        ]

    def last_sum(m):
        mine = z_one[m][z_hi].astype(F32) + held_z[m][z_hi, z_lo].astype(F32)
        finish(flight[m, 4])
        total = mine + z_two[m][...].astype(F32)
        out = grad_refs[m]
        deep, wide = out.shape
        if m == G_IN:
            out[:, : wide // 2] = total[:deep, :]
            out[:, wide // 2 :] = total[deep:, :]
        else:
            out[...] = total[:, :wide]

    peers = (to_core, to_x, to_y, to_z_lo, to_z_hi)

    def vector_start(g):
        vec_own[g, 0] = jnp.transpose(vec_cols[...])[8 * g : 8 * g + 8, :]
        flight["v", g] = remote(
            vec_own.at[g, 0], vec_in.at[g, 0], peers[0], v_send.at[g, 0], v_recv.at[g, 0]
        )

    def vector_step(g, k):
        flight["v", g].wait()
        total = vec_own[g, k] + vec_in[g, k]
        if k == 4:
            vecs_ref[8 * g : 8 * g + 8, :] = total
        else:
            vec_own[g, k + 1] = total
            flight["v", g] = remote(
                vec_own.at[g, k + 1],
                vec_in.at[g, k + 1],
                peers[k + 1],
                v_send.at[g, k + 1],
                v_recv.at[g, k + 1],
            )

    if fused:
        first_start()
        for m in (G_OUT, G_O, G_QKV):
            held_z[m][...] = jnp.zeros_like(held_z[m])
        pool_own[...] = jnp.transpose(jnp.broadcast_to(pooled_col, (width, 128)))[0:8, :]
        pool_in[me_s] = pool_own[...]
        flight["p"] = [
            remote(pool_own, pool_in.at[me_s], seq_peer(d), p_send.at[d], p_recv.at[d])
            for d in range(1, seq_count)
        ]
        first_add()
    else:
        vec_cols[:, 12:13] = pooled_col
        put(G_OUT)

    for i in range(parts):
        rows = slice(i * width, (i + 1) * width)
        grad_act_low = nn(w_out[rows, :], low_a[...]).astype(BF)
        grad_pre = (grad_act_low.astype(F32) * slope[rows, :].astype(F32)).astype(BF)
        slope[rows, :] = grad_pre
        vec_cols[:, 3 + i : 4 + i] = jnp.sum(grad_pre.astype(F32), 1, keepdims=True)
    if fused:
        to_core_start(G_IN)
    else:
        put(G_IN)
    grad_middle = grad_second[...] + nn(w_in[...], slope[...])

    vec_cols[:, 7:8] = jnp.sum(grad_middle * normed_one[...], 1, keepdims=True)
    vec_cols[:, 8:9] = jnp.sum(grad_middle, 1, keepdims=True)
    grad_first = normed_two
    grad_first[...] = norm_back(grad_middle * column(V_G1), normed_one[...], inv_one)
    low_a[...] = grad_first[...].astype(BF)
    vec_cols[:, 9:10] = jnp.sum(low_a[...].astype(F32), 1, keepdims=True)
    if fused:
        to_core_add(G_IN)
        to_core_start(G_O)
        vector_start(0)
    else:
        put(G_O)
    grad_heads = nn(w_o[...], low_a[...])
    for h in range(H):
        rows = slice(h * head, (h + 1) * head)
        grad_att[rows, :] = (grad_heads[rows, :] * inv_sum[h * 8 : h * 8 + 1, :]).astype(BF)
    if fused:
        second_link(G_OUT)
        to_core_add(G_O)
        vector_step(0, 0)

    def attend_back(h, carry):
        grad = grad_att[head_rows(h, 0), :]
        inner = jnp.sum(grad.astype(F32) * att_t[head_rows(h, 0), :].astype(F32), 0, keepdims=True)
        weights_low = expo[aligned(h, seq_len), :]
        queries, keys, values = (qkv_t[head_rows(h, third), :] for third in range(3))
        grad_probs = tn(values, grad)
        grad_scores = (weights_low.astype(F32) * (grad_probs - inner)).astype(BF)
        qkv_t[head_rows(h, 0), :] = (nn(keys, grad_scores) * scale).astype(BF)
        qkv_t[head_rows(h, 1), :] = nt(queries, grad_scores).astype(BF)
        qkv_t[head_rows(h, 2), :] = nt(grad, weights_low).astype(BF)
        return carry

    if fused:
        for k in range(3):
            lax.fori_loop(k * (H // 3), (k + 1) * (H // 3), attend_back, 0)
            vector_step(0, k + 1)
    else:
        lax.fori_loop(0, H, attend_back, 0)
    vec_cols[:, 10:11] = jnp.sum(qkv_t[0:width, :].astype(F32), 1, keepdims=True)
    vec_cols[:, 11:12] = jnp.sum(qkv_t[2 * width :, :].astype(F32), 1, keepdims=True)
    if fused:
        to_core_start(G_QKV)
        vector_start(1)
        vector_step(0, 4)
    grad_in = nn(w_qkv[...], qkv_t[...]) + grad_first[...]
    rows_gin = cot_rows
    rows_gin[...] = jnp.transpose(grad_in.astype(BF)).reshape(seq_count, block_len, width)
    gin_copies = exchange(rows_gin, gin_ref, 3, g_send, g_recv)
    if fused:
        to_core_add(G_QKV)
        vector_step(1, 0)
        second_link(G_IN)
        first_z(G_OUT)
        second_link(G_O)
        vector_step(1, 1)
        second_z(G_OUT)
        second_link(G_QKV)
        first_z(G_IN)
        last_sum(G_OUT)
        first_z(G_O)
        vector_step(1, 2)
        second_z(G_IN)
        second_z(G_O)
        last_sum(G_IN)
        first_z(G_QKV)
        last_sum(G_O)
        vector_step(1, 3)
        second_z(G_QKV)
        vector_step(1, 4)
        finish(flight["p"])
        for k in range(seq_count):
            pooled_ref[k : k + 1, :] = pool_in[k, 0:1, :]
        last_sum(G_QKV)
        for copy in flight[G_OUT, 0]:
            pass
    else:
        put(G_QKV)
        vecs_ref[...] = jnp.transpose(vec_cols[...])[0:16, :]
        pooled_ref[...] = jnp.transpose(vec_cols[...])[12:16, :]
    finish(out_copies)
    finish(gin_copies)


def body(
    hidden_in,
    lengths,
    w_qkv,
    b_q,
    b_v,
    w_o,
    b_o,
    gain_one,
    shift_one,
    w_in,
    b_in,
    w_out,
    b_out,
    gain_two,
    shift_two,
    cot_hidden,
    cot_pooled,
):
    batch_count, seq_count = lax.axis_size("batch"), lax.axis_size("seq")
    seqs_here, block_len, width = hidden_in.shape
    ff = w_in.shape[1]
    seq_len = seq_count * block_len
    assert seqs_here == seq_count
    fused = batch_count == 8 and seq_count == 4

    anywhere = pl.BlockSpec(memory_space=pl.ANY)
    vmem = pl.BlockSpec(memory_space=pltpu.VMEM)
    smem = pl.BlockSpec(memory_space=pltpu.SMEM)
    rows = jax.ShapeDtypeStruct(hidden_in.shape, BF)
    weights = (w_out, w_in, w_o, w_qkv)
    if fused:
        grads = tuple(
            jax.ShapeDtypeStruct((w.shape[0] // batch_count, w.shape[1] // seq_count), F32)
            for w in weights
        )
    else:
        grads = tuple(jax.ShapeDtypeStruct(w.shape, BF) for w in weights)
    dma = pltpu.SemaphoreType.DMA
    scratch = [pltpu.VMEM(w.shape, BF) for w in (w_qkv, w_o, w_in, w_out)]
    scratch += [
        pltpu.VMEM((seq_count, block_len, width), BF),
        pltpu.VMEM((seq_count, block_len, width), BF),
        pltpu.VMEM((width, seq_len), BF),
        pltpu.VMEM((3 * width, seq_len), BF),
        pltpu.VMEM((H * seq_len, seq_len), BF),
        pltpu.VMEM((H * 8, seq_len), F32),
        pltpu.VMEM((width, seq_len), BF),
        pltpu.VMEM((width, seq_len), F32),
        pltpu.VMEM((width, seq_len), BF),
        pltpu.VMEM((ff, seq_len), BF),
        pltpu.VMEM((ff, seq_len), BF),
        pltpu.VMEM((width, seq_len), F32),
        pltpu.VMEM((width, seq_len), F32),
        pltpu.VMEM((width, seq_len), BF),
        pltpu.VMEM((width, seq_len), BF),
        pltpu.VMEM((width, 128), F32),
        dma((4,)),
        dma((4,)),
    ]
    scratch += [dma((seq_count,))] * 8
    if fused:
        deep = width // batch_count
        blocks = (
            (ff // batch_count, width // 2),
            (deep * (ff // width), width // 2),
            (deep, width // 2),
            (deep, 3 * width // 2),
        )
        wide = [-(-w.shape[1] // seq_count // 128) * 128 for w in weights]
        z_blocks = (
            (ff // batch_count, wide[0]),
            (deep * (ff // width) // 2, width // 2),
            (deep, wide[2]),
            (deep, wide[3]),
        )
        scratch += [pltpu.VMEM((2, 2, 2) + blocks[m], BF) for m in (0, 2, 3)]
        scratch += [pltpu.VMEM((2, 2, 2) + block, BF) for block in blocks]
        scratch += [pltpu.VMEM((2, 2) + block, BF) for block in blocks]
        scratch += [pltpu.VMEM((2,) + block, BF) for block in blocks]
        scratch += [pltpu.VMEM((2, 2) + block, BF) for block in z_blocks]
        scratch += [pltpu.VMEM((2,) + block, BF) for block in z_blocks]
        scratch += [pltpu.VMEM(block, BF) for block in z_blocks]
        scratch += [dma((4, 4)), dma((4, 4)), dma((4, 8)), dma((4, 8))]
        scratch += [
            pltpu.VMEM((2, 5, 8, width), F32),
            pltpu.VMEM((2, 5, 8, width), F32),
            pltpu.VMEM((8, width), F32),
            pltpu.VMEM((seq_count, 8, width), F32),
            dma((2, 5)),
            dma((2, 5)),
            dma((seq_count,)),
            dma((seq_count,)),
        ]
    else:
        scratch += [pltpu.VMEM((width, ff), BF), dma((1,))]
    outs = pl.pallas_call(
        functools.partial(
            layer_kernel, (batch_count, seq_count, block_len, width, ff, fused)
        ),
        out_shape=(
            rows,
            rows,
            jax.ShapeDtypeStruct((seq_count, width), F32),
            jax.ShapeDtypeStruct((16, width), F32),
        )
        + grads,
        in_specs=[anywhere, anywhere, smem] + [vmem] * 10 + [anywhere] * 4,
        out_specs=(anywhere, anywhere, vmem, vmem) + (vmem if fused else anywhere,) * 4,
        scratch_shapes=scratch,
        compiler_params=pltpu.CompilerParams(
            collective_id=0, has_side_effects=True, vmem_limit_bytes=63 * 2**20
        ),
        name="encoder_layer",
    )(
        hidden_in,
        cot_hidden,
        lengths,
        cot_pooled,
        b_q,
        b_v,
        b_o,
        gain_one,
        shift_one,
        b_out,
        gain_two,
        shift_two,
        b_in,
        w_qkv,
        w_o,
        w_in,
        w_out,
    )
    out_hidden, grad_in, pooled, total, g_out, g_in, g_o, g_qkv = outs
    if not fused:
        pooled = lax.all_gather(pooled[0], "seq", axis=0)
        total = lax.psum(total[:12], ("batch", "seq"))

        def scatter(grad):
            part = lax.psum_scatter(grad.astype(F32), "batch", scatter_dimension=0, tiled=True)
            part = lax.psum_scatter(part.astype(BF), "seq", scatter_dimension=1, tiled=True)
            return part.astype(F32)

        g_out, g_in, g_o, g_qkv = (scatter(g) for g in (g_out, g_in, g_o, g_qkv))
    return (
        out_hidden,
        pooled,
        grad_in,
        g_qkv,
        total[10],
        total[11],
        g_o,
        total[9],
        total[7],
        total[8],
        g_in,
        total[3:7].reshape(ff),
        g_out,
        total[2],
        total[0],
        total[1],
    )


def solution(mesh):
    rows = P("batch", "seq", None)
    shard = P("batch", "seq")
    in_specs = (rows, P("batch")) + (P(),) * 13 + (rows, P("batch", None))
    out_specs = (
        rows,
        P("batch", None),
        rows,
        shard,
        P(),
        P(),
        shard,
        P(),
        P(),
        P(),
        shard,
        P(),
        shard,
        P(),
        P(),
        P(),
    )
    return jax.shard_map(body, mesh=mesh, in_specs=in_specs, out_specs=out_specs, check_vma=False)
```

time: 423 us -> 173 us (0.41)
  waiting for transfers between devices: 233 us -> 0 us
  Pallas kernels: 94.3 us -> 157 us
  blocking collectives: 52.8 us -> 0 us
  between operations: 14.3 us -> 0.68 us
  local copies, waits for them, and re-layouts: 24.6 us -> 14.2 us
    reduce_scatter x5 -> x0, waiting for transfers between devices: 221 us -> none  [the longest x4 200 us: scatter(): lax.psum_scatter(grad.astype(F32), 'batch', scatter_dimension=0, tiled=True)]
    pallas_call x1, Pallas kernels: 94.3 us -> 157 us  [body(): pl.pallas_call(functools.partial(layer_kernel, (batch_count, seq_count, b...]
    psum x1 -> x0, blocking collectives: 39.7 us -> none  [body(): total = lax.psum(vecs[:12], ('batch', 'seq'))]
    all_gather x1 -> x0, blocking collectives: 13.1 us -> none  [body(): pooled = lax.all_gather(pooled_row[4], 'seq', axis=0)]
    unnamed x11 -> x0, waiting for transfers between devices: 11.4 us -> none
    unnamed x28 -> x9, local copies, waits for them, and re-layouts: 20.5 us -> 11.2 us
  transfers between devices with their start and end apart: 8 -> 0, of which waited for: 6 -> 0; matrix products, arithmetic and copies ran while one was open for 3% -> 0% of each run, Pallas kernels for 0% -> 0%
where the time goes in v2:
time: 173 us; the launch traced here: 172 us
  Pallas kernels  157 us (91%)
  local copies, waits for them, and re-layouts  14.2 us (8%)
    pallas_call x1, Pallas kernels, body(): pl.pallas_call(functools.partial(layer_kernel, (batch_count, seq_count, b...  157 us
    unnamed x9, local copies, waits for them, and re-layouts  11.2 us

profile of v2, /device:TPU:0, one launch (start us, length us, event | category | flops | bytes accessed | tf_op | source)
XLA Modules:
  0.0 172.2 jit_solution(13125768509733738393)
XLA Ops:
  0.7 157.3 %encoder_layer.1 = (bf16[4,128,768]{2,1,0:T(8,128)(2,1)}, bf16[4,128,768]{2,1,0:T(8,128)(2,1)}, f32[4,768]{1,0:T(4,128)}, f32[16,768]{1,0:T(8,128)}, f32[384,192...) custom-call(bf16[4,128,768]{2,1,0:T(8,128)(2,1)} %refs_0_.1, ...), custom_call_target="tpu_custom_call" | custom-call | tf_op jit(solution)/shard_map/encoder_layer/pallas_call | solution.py:644
  158.0 0.0 copy-start
  158.0 1.6 slice_reduce_fusion
  159.6 0.7 slice.32
  160.4 0.6 reshape.35
  161.0 1.9 %copy.33 = f32[384,192]{0,1:T(8,128)} copy(f32[384,192]{1,0:T(8,128)} %get-tuple-element.44) | data formatting | bytes 589824
  162.8 2.1 %copy.40 = bf16[4,128,768]{2,1,0:T(8,128)(2,1)} copy(bf16[4,128,768]{2,1,0:T(8,128)(2,1)} %get-tuple-element.72) | data formatting | bytes 1572864
  164.9 1.3 copy.41
  166.2 2.1 %copy.42 = bf16[4,128,768]{2,1,0:T(8,128)(2,1)} copy(bf16[4,128,768]{2,1,0:T(8,128)(2,1)} %get-tuple-element.74) | data formatting | bytes 1572864
  168.3 1.7 copy.43
  169.9 1.5 copy.44
  171.5 0.0 copy-done
  171.5 0.7 copy.45
Async XLA Ops:
  158.0 13.5 %copy-start = (f32[96,768]{1,0:T(8,128)S(1)}, f32[96,768]{1,0:T(8,128)}, u32[]{:S(2)}) copy-start(f32[96,768]{1,0:T(8,128)} %get-tuple-element.82) | copy-start | bytes 884740

commit v3 on v2

--- a/solution.py
+++ b/solution.py
@@ -63,7 +63,7 @@
     vec_cols, w_sem, own_sem = take(3)
     x_send, x_recv, c_send, c_recv, o_send, o_recv, g_send, g_recv = take(8)
     if fused:
-        send_core = take(3)
+        (send_core,) = take(1)
         held_core, held_one, held_two, held_z, z_one, z_two = (take(4) for _ in range(6))
         core_send, core_recv, link_send, link_recv = take(4)
         vec_own, vec_in, pool_own, pool_in, v_send, v_recv, p_send, p_recv = take(8)
@@ -201,20 +201,11 @@
     centred = summed - jnp.mean(summed, 0, keepdims=True)
     inv_two = lax.rsqrt(jnp.mean(centred * centred, 0, keepdims=True) + 1e-12)
     normed_two[...] = centred * inv_two
-    output = normed_two[...] * column(V_G2) + column(V_S2)
-    pooled_col = jnp.sum(output * (live * inv_len), 1, keepdims=True)
-    rows_out = x_rows
-    rows_out[...] = jnp.transpose(output.astype(BF)).reshape(seq_count, block_len, width)
-    out_copies = exchange(rows_out, out_ref, 2, o_send, o_recv)
-
     finish(cot_copies)
     grad_final = jnp.transpose(cot_rows[...].reshape(seq_len, width)).astype(F32)
     grad_final = grad_final + column(V_CP) * (live * inv_len)
-    vec_cols[:, 0:1] = jnp.sum(grad_final * normed_two[...], 1, keepdims=True)
-    vec_cols[:, 1:2] = jnp.sum(grad_final, 1, keepdims=True)
     grad_second[...] = norm_back(grad_final * column(V_G2), normed_two[...], inv_two)
     low_a[...] = grad_second[...].astype(BF)
-    vec_cols[:, 2:3] = jnp.sum(low_a[...].astype(F32), 1, keepdims=True)
 
     def whole_grad(m):
         if m == G_OUT:
@@ -244,24 +235,28 @@
     def partial(m, which):
         rows, columns = whole_grad(m)
         deep = rows.shape[0] // batch_count
-        picked = [rows[aligned(2 * j + which, deep), :] for j in range(4)]
-        value = nt(jnp.concatenate(picked, 0), columns[...])
-        half = value.shape[1] // 2
-        tile = half // parts if m == G_IN else half
-        for j in range(4):
-            for h in range(2):
+        left = jnp.concatenate([rows[aligned(2 * j + which, deep), :] for j in range(4)], 0)
+        tile = width // 2
+        half = columns.shape[0] // 2
+        for h in range(2):
+            value = nt(left, columns[h * half : (h + 1) * half, :])
+            for j in range(4):
                 for t in range(half // tile):
-                    start = h * half + t * tile
-                    block = value[j * deep : (j + 1) * deep, start : start + tile]
+                    block = value[j * deep : (j + 1) * deep, t * tile : (t + 1) * tile]
                     yield h, j, slice(t * deep, (t + 1) * deep), block
 
     def core_buffer(m):
-        return send_core[max(m - 1, 0)]
-
-    def to_core_start(m):
+        rows = held_core[m].shape[3]
+        start = held_core[G_O].shape[3] if m == G_QKV else 0
+        return send_core.at[:, :, :, start : start + rows, :]
+
+    def core_start(m):
         buffer = core_buffer(m)
         if m == G_IN:
             for copy in flight[G_OUT, 0]:
+                copy.wait_send()
+        if m == G_O:
+            for copy in flight[G_IN, 0]:
                 copy.wait_send()
         for h, j, rows, block in partial(m, 1 - core):
             buffer[h, j // 2, j % 2, rows, :] = block.astype(BF)
@@ -269,11 +264,17 @@
             remote(buffer, held_core[m], to_core, core_send.at[m, 0], core_recv.at[m, 0])
         ]
 
-    def to_core_add(m):
-        finish(flight[m, 0]) if m != G_OUT else None
+    def core_add(m):
+        for copy in flight[m, 0]:
+            copy.wait_recv()
+            if m in (G_O, G_QKV):
+                copy.wait_send()
         held = held_core[m]
         for h, j, rows, block in partial(m, core):
             held[h, j // 2, j % 2, rows, :] = add_low(held[h, j // 2, j % 2, rows, :], block)
+
+    def first_link(m):
+        held = held_core[m]
         flight[m, 1] = [
             remote(
                 held.at[0, :, 1 - at_x],
@@ -299,7 +300,7 @@
         return nt(act[row, :], low_a[...])
 
     def first_start():
-        buffer = send_core[0]
+        buffer = send_core
         copies = []
         for k, (y, x) in enumerate(order):
             value = first_block(y, x, 1 - core)
@@ -377,13 +378,32 @@
         after, last, ready = held_one[m], held_two[m], held_z[m]
         for h in range(2):
             mine = after[0, at_y] if h == 0 else after[1, at_x]
-            block = add_low(last[h], mine)
-            deep, wide = block.shape
+            block = last[h].astype(F32) + mine.astype(F32)
+            if m == G_IN:
+                deep = block.shape[0] // 2
+                for k in range(2):
+                    ready[h, k] = block[k * deep : (k + 1) * deep, :].astype(BF)
+                continue
+            deep = grad_refs[m].shape[0]
+            per_row = width // 256
+            count = block.shape[0] // deep * per_row
+            tiles = []
+            for t in range(count):
+                row, lane = t // per_row * deep, t % per_row * 128
+                tiles.append(block[row : row + deep, lane : lane + 128])
+            full = count // 2
             for k in range(2):
-                if m == G_IN:
-                    ready[h, k] = block[k * (deep // 2) : (k + 1) * (deep // 2), :]
-                else:
-                    ready[h, k, :, : wide // 2] = block[:, k * (wide // 2) : (k + 1) * (wide // 2)]
+                for t in range(full):
+                    ready[h, k, t * deep : (t + 1) * deep, :] = tiles[t + k * (full + 1)].astype(BF)
+            turned = pltpu.roll(tiles[full], 64, 1)
+            left = lax.broadcasted_iota(jnp.int32, (deep // 2, 128), 1) < 64
+            upper, lower = slice(0, deep // 2), slice(deep // 2, deep)
+            folded = (
+                jnp.where(left, tiles[full][upper], turned[lower]),
+                jnp.where(left, turned[upper], tiles[full][lower]),
+            )
+            for k in range(2):
+                ready[h, k, full * deep :, :] = folded[k].astype(BF)
         flight[m, 3] = [
             remote(
                 ready.at[:, 1 - z_lo], z_one[m], to_z_lo, link_send.at[m, 6], link_recv.at[m, 6]
@@ -408,46 +428,62 @@
         if m == G_IN:
             out[:, : wide // 2] = total[:deep, :]
             out[:, wide // 2 :] = total[deep:, :]
+            return
+        full = wide // 128
+        tiles = [total[t * deep : (t + 1) * deep, :] for t in range(full)]
+        folded = total[full * deep :, :]
+        turned = pltpu.roll(folded, 64, 1)
+        after_tiles = jnp.concatenate(tiles + [jnp.concatenate([folded, turned], 0)], 1)
+        before_tiles = jnp.concatenate([jnp.concatenate([turned, folded], 0)] + tiles, 1)
+        before_tiles = pltpu.roll(before_tiles, full * 128 + 64, 1)
+        out[...] = jnp.where(z_lo == 0, after_tiles, before_tiles)[:, :wide]
+
+    peers = (to_core, to_x, to_y, to_z_lo, to_z_hi)
+
+    def vector_start():
+        vec_own[0] = jnp.transpose(vec_cols[...])[0:16, :]
+        flight["v"] = remote(vec_own.at[0], vec_in.at[0], peers[0], v_send.at[0], v_recv.at[0])
+
+    def vector_step(k):
+        flight["v"].wait()
+        total = vec_own[k] + vec_in[k]
+        if k == 4:
+            vecs_ref[...] = total
         else:
-            out[...] = total[:, :wide]
-
-    peers = (to_core, to_x, to_y, to_z_lo, to_z_hi)
-
-    def vector_start(g):
-        vec_own[g, 0] = jnp.transpose(vec_cols[...])[8 * g : 8 * g + 8, :]
-        flight["v", g] = remote(
-            vec_own.at[g, 0], vec_in.at[g, 0], peers[0], v_send.at[g, 0], v_recv.at[g, 0]
-        )
-
-    def vector_step(g, k):
-        flight["v", g].wait()
-        total = vec_own[g, k] + vec_in[g, k]
-        if k == 4:
-            vecs_ref[8 * g : 8 * g + 8, :] = total
-        else:
-            vec_own[g, k + 1] = total
-            flight["v", g] = remote(
-                vec_own.at[g, k + 1],
-                vec_in.at[g, k + 1],
+            vec_own[k + 1] = total
+            flight["v"] = remote(
+                vec_own.at[k + 1],
+                vec_in.at[k + 1],
                 peers[k + 1],
-                v_send.at[g, k + 1],
-                v_recv.at[g, k + 1],
+                v_send.at[k + 1],
+                v_recv.at[k + 1],
             )
 
     if fused:
         first_start()
-        for m in (G_OUT, G_O, G_QKV):
-            held_z[m][...] = jnp.zeros_like(held_z[m])
+        first_add()
+    else:
+        put(G_OUT)
+
+    rows_out = x_rows
+    output = normed_two[...] * column(V_G2) + column(V_S2)
+    rows_out[...] = jnp.transpose(output.astype(BF)).reshape(seq_count, block_len, width)
+    out_copies = exchange(rows_out, out_ref, 2, o_send, o_recv)
+    pooled_col = jnp.sum(output * (live * inv_len), 1, keepdims=True)
+    if fused:
         pool_own[...] = jnp.transpose(jnp.broadcast_to(pooled_col, (width, 128)))[0:8, :]
         pool_in[me_s] = pool_own[...]
         flight["p"] = [
             remote(pool_own, pool_in.at[me_s], seq_peer(d), p_send.at[d], p_recv.at[d])
             for d in range(1, seq_count)
         ]
-        first_add()
     else:
         vec_cols[:, 12:13] = pooled_col
-        put(G_OUT)
+    grad_final = jnp.transpose(cot_rows[...].reshape(seq_len, width)).astype(F32)
+    grad_final = grad_final + column(V_CP) * (live * inv_len)
+    vec_cols[:, 0:1] = jnp.sum(grad_final * normed_two[...], 1, keepdims=True)
+    vec_cols[:, 1:2] = jnp.sum(grad_final, 1, keepdims=True)
+    vec_cols[:, 2:3] = jnp.sum(low_a[...].astype(F32), 1, keepdims=True)
 
     for i in range(parts):
         rows = slice(i * width, (i + 1) * width)
@@ -456,7 +492,7 @@
         slope[rows, :] = grad_pre
         vec_cols[:, 3 + i : 4 + i] = jnp.sum(grad_pre.astype(F32), 1, keepdims=True)
     if fused:
-        to_core_start(G_IN)
+        core_start(G_IN)
     else:
         put(G_IN)
     grad_middle = grad_second[...] + nn(w_in[...], slope[...])
@@ -468,9 +504,10 @@
     low_a[...] = grad_first[...].astype(BF)
     vec_cols[:, 9:10] = jnp.sum(low_a[...].astype(F32), 1, keepdims=True)
     if fused:
-        to_core_add(G_IN)
-        to_core_start(G_O)
-        vector_start(0)
+        second_link(G_OUT)
+        core_add(G_IN)
+        first_link(G_IN)
+        core_start(G_O)
     else:
         put(G_O)
     grad_heads = nn(w_o[...], low_a[...])
@@ -478,9 +515,7 @@
         rows = slice(h * head, (h + 1) * head)
         grad_att[rows, :] = (grad_heads[rows, :] * inv_sum[h * 8 : h * 8 + 1, :]).astype(BF)
     if fused:
-        second_link(G_OUT)
-        to_core_add(G_O)
-        vector_step(0, 0)
+        core_add(G_O)
 
     def attend_back(h, carry):
         grad = grad_att[head_rows(h, 0), :]
@@ -497,52 +532,105 @@
     if fused:
         for k in range(3):
             lax.fori_loop(k * (H // 3), (k + 1) * (H // 3), attend_back, 0)
-            vector_step(0, k + 1)
+            if k == 0:
+                first_z(G_OUT)
+            if k == 2:
+                second_z(G_OUT)
     else:
         lax.fori_loop(0, H, attend_back, 0)
     vec_cols[:, 10:11] = jnp.sum(qkv_t[0:width, :].astype(F32), 1, keepdims=True)
     vec_cols[:, 11:12] = jnp.sum(qkv_t[2 * width :, :].astype(F32), 1, keepdims=True)
     if fused:
-        to_core_start(G_QKV)
-        vector_start(1)
-        vector_step(0, 4)
+        vector_start()
+        core_start(G_QKV)
     grad_in = nn(w_qkv[...], qkv_t[...]) + grad_first[...]
     rows_gin = cot_rows
     rows_gin[...] = jnp.transpose(grad_in.astype(BF)).reshape(seq_count, block_len, width)
     gin_copies = exchange(rows_gin, gin_ref, 3, g_send, g_recv)
     if fused:
-        to_core_add(G_QKV)
-        vector_step(1, 0)
+        core_add(G_QKV)
         second_link(G_IN)
-        first_z(G_OUT)
-        second_link(G_O)
-        vector_step(1, 1)
-        second_z(G_OUT)
-        second_link(G_QKV)
+        vector_step(0)
+        first_link(G_QKV)
+        first_link(G_O)
         first_z(G_IN)
         last_sum(G_OUT)
+        vector_step(1)
+        second_link(G_QKV)
+        second_link(G_O)
+        second_z(G_IN)
+        vector_step(2)
+        first_z(G_QKV)
         first_z(G_O)
-        vector_step(1, 2)
-        second_z(G_IN)
+        last_sum(G_IN)
+        vector_step(3)
+        second_z(G_QKV)
         second_z(G_O)
-        last_sum(G_IN)
-        first_z(G_QKV)
-        last_sum(G_O)
-        vector_step(1, 3)
-        second_z(G_QKV)
-        vector_step(1, 4)
         finish(flight["p"])
         for k in range(seq_count):
             pooled_ref[k : k + 1, :] = pool_in[k, 0:1, :]
+        vector_step(4)
         last_sum(G_QKV)
-        for copy in flight[G_OUT, 0]:
-            pass
+        last_sum(G_O)
     else:
         put(G_QKV)
         vecs_ref[...] = jnp.transpose(vec_cols[...])[0:16, :]
         pooled_ref[...] = jnp.transpose(vec_cols[...])[12:16, :]
     finish(out_copies)
     finish(gin_copies)
+
+
+def deliver_kernel(*refs):
+    out_in, gin_in, pooled_in, vecs_in = refs[:4]
+    grads_in = refs[4:8]
+    out_ref, gin_ref, pooled_ref = refs[8:11]
+    grad_refs, vec_refs = refs[11:15], refs[15:24]
+    grad_refs[0][...] = jnp.transpose(grads_in[0][...])
+    moves = [(out_in, out_ref), (gin_in, gin_ref), (pooled_in, pooled_ref)]
+    for src, dst in moves + list(zip(grads_in[1:], grad_refs[1:])):
+        dst[...] = src[...]
+    width = vecs_in.shape[1]
+    for row, ref in zip((10, 11, 9, 7, 8, 3, 2, 0, 1), vec_refs):
+        for i in range(ref.shape[0] // width):
+            ref[i * width : (i + 1) * width] = vecs_in[row + i : row + i + 1, :].reshape(width)
+
+
+def deliver(outs):
+    out_hidden, grad_in, pooled, total, g_out, g_in, g_o, g_qkv = outs
+    ff = total.shape[1] * g_out.shape[0] // g_qkv.shape[0]
+    vmem = pl.BlockSpec(memory_space=pltpu.VMEM)
+    arrays = (out_hidden, grad_in, pooled, g_out, g_in, g_o, g_qkv)
+    lengths = [total.shape[1]] * 5 + [ff] + [total.shape[1]] * 3
+    vectors = tuple(jax.ShapeDtypeStruct((n,), F32) for n in lengths)
+    shapes = [jax.ShapeDtypeStruct(a.shape, a.dtype) for a in arrays]
+    shapes[3] = jax.ShapeDtypeStruct(g_out.shape[::-1], F32)
+    results = pl.pallas_call(
+        deliver_kernel,
+        out_shape=tuple(shapes) + vectors,
+        in_specs=[vmem] * 8,
+        out_specs=(vmem,) * 16,
+        name="deliver",
+    )(*outs)
+    out_hidden, grad_in, pooled, g_out, g_in, g_o, g_qkv = results[:7]
+    b_q, b_v, b_o, gain_one, shift_one, b_in, b_out, gain_two, shift_two = results[7:]
+    return (
+        out_hidden,
+        pooled,
+        grad_in,
+        g_qkv,
+        b_q,
+        b_v,
+        g_o,
+        b_o,
+        gain_one,
+        shift_one,
+        g_in,
+        b_in,
+        g_out.T,
+        b_out,
+        gain_two,
+        shift_two,
+    )
 
 
 def body(
@@ -612,16 +700,13 @@
             (ff // batch_count, width // 2),
             (deep * (ff // width), width // 2),
             (deep, width // 2),
-            (deep, 3 * width // 2),
+            (deep * 3, width // 2),
         )
-        wide = [-(-w.shape[1] // seq_count // 128) * 128 for w in weights]
-        z_blocks = (
-            (ff // batch_count, wide[0]),
-            (deep * (ff // width) // 2, width // 2),
-            (deep, wide[2]),
-            (deep, wide[3]),
+        z_blocks = tuple(
+            (block[0] // 2, block[1]) if m == G_IN else (block[0] * block[1] // 256, 128)
+            for m, block in enumerate(blocks)
         )
-        scratch += [pltpu.VMEM((2, 2, 2) + blocks[m], BF) for m in (0, 2, 3)]
+        scratch += [pltpu.VMEM((2, 2, 2) + blocks[0], BF)]
         scratch += [pltpu.VMEM((2, 2, 2) + block, BF) for block in blocks]
         scratch += [pltpu.VMEM((2, 2) + block, BF) for block in blocks]
         scratch += [pltpu.VMEM((2,) + block, BF) for block in blocks]
@@ -630,12 +715,12 @@
         scratch += [pltpu.VMEM(block, BF) for block in z_blocks]
         scratch += [dma((4, 4)), dma((4, 4)), dma((4, 8)), dma((4, 8))]
         scratch += [
-            pltpu.VMEM((2, 5, 8, width), F32),
-            pltpu.VMEM((2, 5, 8, width), F32),
+            pltpu.VMEM((5, 16, width), F32),
+            pltpu.VMEM((5, 16, width), F32),
             pltpu.VMEM((8, width), F32),
             pltpu.VMEM((seq_count, 8, width), F32),
-            dma((2, 5)),
-            dma((2, 5)),
+            dma((5,)),
+            dma((5,)),
             dma((seq_count,)),
             dma((seq_count,)),
         ]
@@ -678,17 +763,18 @@
         w_in,
         w_out,
     )
+    if fused:
+        return deliver(outs)
     out_hidden, grad_in, pooled, total, g_out, g_in, g_o, g_qkv = outs
-    if not fused:
-        pooled = lax.all_gather(pooled[0], "seq", axis=0)
-        total = lax.psum(total[:12], ("batch", "seq"))
-
-        def scatter(grad):
-            part = lax.psum_scatter(grad.astype(F32), "batch", scatter_dimension=0, tiled=True)
-            part = lax.psum_scatter(part.astype(BF), "seq", scatter_dimension=1, tiled=True)
-            return part.astype(F32)
-
-        g_out, g_in, g_o, g_qkv = (scatter(g) for g in (g_out, g_in, g_o, g_qkv))
+    pooled = lax.all_gather(pooled[0], "seq", axis=0)
+    total = lax.psum(total[:12], ("batch", "seq"))
+
+    def scatter(grad):
+        part = lax.psum_scatter(grad.astype(F32), "batch", scatter_dimension=0, tiled=True)
+        part = lax.psum_scatter(part.astype(BF), "seq", scatter_dimension=1, tiled=True)
+        return part.astype(F32)
+
+    g_out, g_in, g_o, g_qkv = (scatter(g) for g in (g_out, g_in, g_o, g_qkv))
     return (
         out_hidden,
         pooled,

time: 173 us -> 137 us (0.79)
  Pallas kernels: 157 us -> 136 us
  local copies, waits for them, and re-layouts: 14.2 us -> 0 us
    pallas_call x1, Pallas kernels: 157 us -> 132 us  [body(): pl.pallas_call(functools.partial(layer_kernel, (batch_count, seq_count, b...]
    unnamed x9 -> x0, local copies, waits for them, and re-layouts: 11.2 us -> none
    pallas_call x0 -> x1, Pallas kernels: none -> 3.29 us  [deliver(): pl.pallas_call(deliver_kernel, out_shape=tuple(shapes) + vectors, in_spec...]
    slice x2 -> x0, local copies, waits for them, and re-layouts: 2.39 us -> none  [the longest x1 1.65 us: body(): total[1]]
where the time goes in v3:
time: 137 us
  Pallas kernels  136 us (99%)
    pallas_call x1, Pallas kernels, body(): pl.pallas_call(functools.partial(layer_kernel, (batch_count, seq_count, b...  132 us
    pallas_call x1, Pallas kernels, deliver(): pl.pallas_call(deliver_kernel, out_shape=tuple(shapes) + vectors, in_spec...  3.29 us

profile of v3, /device:TPU:0, one launch (start us, length us, event | category | flops | bytes accessed | tf_op | source)
XLA Modules:
  0.0 136.6 jit_solution(10260192560626008377)
XLA Ops:
  0.7 132.4 %encoder_layer.1 = (bf16[4,128,768]{2,1,0:T(8,128)(2,1)}, bf16[4,128,768]{2,1,0:T(8,128)(2,1)}, f32[4,768]{1,0:T(4,128)}, f32[16,768]{1,0:T(8,128)}, f32[384,192...) custom-call(bf16[4,128,768]{2,1,0:T(8,128)(2,1)} %refs_0_.1, ...), custom_call_target="tpu_custom_call" | custom-call | tf_op jit(solution)/shard_map/encoder_layer/pallas_call | solution.py:729
  133.1 3.3 %deliver.1 = (bf16[4,128,768]{2,1,0:T(8,128)(2,1)}, bf16[4,128,768]{2,1,0:T(8,128)(2,1)}, f32[4,768]{1,0:T(4,128)}, f32[192,384]{1,0:T(8,128)}, f32[96,768]{1,0:...) custom-call(bf16[4,128,768]{2,1,0:T(8,128)(2,1)} %get-tuple-element., ...), custom_call_target="tpu_custom_call" | custom-call | tf_op jit(solution)/shard_map/deliver/pallas_call | solution.py:607

commit v4 on v3

--- a/solution.py
+++ b/solution.py
@@ -59,7 +59,7 @@
     grad_refs = take(4)
     w_qkv, w_o, w_in, w_out = take(4)
     x_rows, cot_rows, x_t, qkv_t, expo, inv_sum, att_t = take(7)
-    normed_one, middle_low, act, slope, normed_two, grad_second, low_a, grad_att = take(8)
+    normed_one, middle_low, act, slope, normed_two, low_a, grad_att = take(7)
     vec_cols, w_sem, own_sem = take(3)
     x_send, x_recv, c_send, c_recv, o_send, o_recv, g_send, g_recv = take(8)
     if fused:
@@ -204,8 +204,7 @@
     finish(cot_copies)
     grad_final = jnp.transpose(cot_rows[...].reshape(seq_len, width)).astype(F32)
     grad_final = grad_final + column(V_CP) * (live * inv_len)
-    grad_second[...] = norm_back(grad_final * column(V_G2), normed_two[...], inv_two)
-    low_a[...] = grad_second[...].astype(BF)
+    low_a[...] = norm_back(grad_final * column(V_G2), normed_two[...], inv_two).astype(BF)
 
     def whole_grad(m):
         if m == G_OUT:
@@ -299,55 +298,55 @@
         row = aligned(4 * y + 2 * x + which, deep)
         return nt(act[row, :], low_a[...])
 
-    def first_start():
-        buffer = send_core
-        copies = []
-        for k, (y, x) in enumerate(order):
-            value = first_block(y, x, 1 - core)
-            half = value.shape[1] // 2
-            buffer[0, y, x] = value[:, :half].astype(BF)
-            buffer[1, y, x] = value[:, half:].astype(BF)
-            copies.append(
+    def first_send(k):
+        y, x = order[k]
+        value = first_block(y, x, 1 - core)
+        half = value.shape[1] // 2
+        send_core[0, y, x] = value[:, :half].astype(BF)
+        send_core[1, y, x] = value[:, half:].astype(BF)
+        flight[G_OUT, 0].append(
+            remote(
+                send_core.at[:, y, x],
+                held_core[G_OUT].at[:, y, x],
+                to_core,
+                core_send.at[G_OUT, k],
+                core_recv.at[G_OUT, k],
+            )
+        )
+
+    def first_add(k):
+        held, after = held_core[G_OUT], held_one[G_OUT]
+        y, x = order[k]
+        value = first_block(y, x, core)
+        half = value.shape[1] // 2
+        flight[G_OUT, 0][k].wait_recv()
+        held[0, y, x] = add_low(held[0, y, x], value[:, :half])
+        held[1, y, x] = add_low(held[1, y, x], value[:, half:])
+        hops = []
+        if k in (0, 1):
+            hops.append((0, after.at[0, y], to_x, k))
+        if k in (0, 2):
+            hops.append((1, after.at[1, x], to_y, 2 + k // 2))
+        for h, dst, device, sem in hops:
+            flight[G_OUT, 1].append(
                 remote(
-                    buffer.at[:, y, x],
-                    held_core[G_OUT].at[:, y, x],
-                    to_core,
-                    core_send.at[G_OUT, k],
-                    core_recv.at[G_OUT, k],
+                    held.at[h, y, x],
+                    dst,
+                    device,
+                    link_send.at[G_OUT, sem],
+                    link_recv.at[G_OUT, sem],
                 )
             )
-        flight[G_OUT, 0] = copies
-
-    def first_add():
-        held, after = held_core[G_OUT], held_one[G_OUT]
-        copies = []
-        for k, (y, x) in enumerate(order):
-            flight[G_OUT, 0][k].wait_recv()
-            value = first_block(y, x, core)
-            half = value.shape[1] // 2
-            held[0, y, x] = add_low(held[0, y, x], value[:, :half])
-            held[1, y, x] = add_low(held[1, y, x], value[:, half:])
-            if k in (0, 1):
-                copies.append(
-                    remote(
-                        held.at[0, y, x],
-                        after.at[0, y],
-                        to_x,
-                        link_send.at[G_OUT, k],
-                        link_recv.at[G_OUT, k],
-                    )
-                )
-            if k in (0, 2):
-                copies.append(
-                    remote(
-                        held.at[1, y, x],
-                        after.at[1, x],
-                        to_y,
-                        link_send.at[G_OUT, 2 + k // 2],
-                        link_recv.at[G_OUT, 2 + k // 2],
-                    )
-                )
-        flight[G_OUT, 1] = copies
+
+    def first_sums():
+        flight[G_OUT, 0], flight[G_OUT, 1] = [], []
+        first_send(0)
+        first_send(1)
+        first_add(0)
+        first_send(2)
+        first_send(3)
+        for k in range(1, 4):
+            first_add(k)
 
     def second_link(m):
         finish(flight[m, 1])
@@ -460,8 +459,7 @@
             )
 
     if fused:
-        first_start()
-        first_add()
+        first_sums()
     else:
         put(G_OUT)
 
@@ -495,7 +493,9 @@
         core_start(G_IN)
     else:
         put(G_IN)
-    grad_middle = grad_second[...] + nn(w_in[...], slope[...])
+    grad_middle = low_a[...].astype(F32) + nn(w_in[...], slope[...])
+    if fused:
+        second_link(G_OUT)
 
     vec_cols[:, 7:8] = jnp.sum(grad_middle * normed_one[...], 1, keepdims=True)
     vec_cols[:, 8:9] = jnp.sum(grad_middle, 1, keepdims=True)
@@ -504,7 +504,6 @@
     low_a[...] = grad_first[...].astype(BF)
     vec_cols[:, 9:10] = jnp.sum(low_a[...].astype(F32), 1, keepdims=True)
     if fused:
-        second_link(G_OUT)
         core_add(G_IN)
         first_link(G_IN)
         core_start(G_O)
@@ -534,8 +533,6 @@
             lax.fori_loop(k * (H // 3), (k + 1) * (H // 3), attend_back, 0)
             if k == 0:
                 first_z(G_OUT)
-            if k == 2:
-                second_z(G_OUT)
     else:
         lax.fori_loop(0, H, attend_back, 0)
     vec_cols[:, 10:11] = jnp.sum(qkv_t[0:width, :].astype(F32), 1, keepdims=True)
@@ -546,19 +543,21 @@
     grad_in = nn(w_qkv[...], qkv_t[...]) + grad_first[...]
     rows_gin = cot_rows
     rows_gin[...] = jnp.transpose(grad_in.astype(BF)).reshape(seq_count, block_len, width)
+    if fused:
+        second_z(G_OUT)
     gin_copies = exchange(rows_gin, gin_ref, 3, g_send, g_recv)
     if fused:
+        second_link(G_IN)
         core_add(G_QKV)
-        second_link(G_IN)
         vector_step(0)
-        first_link(G_QKV)
         first_link(G_O)
         first_z(G_IN)
+        first_link(G_QKV)
         last_sum(G_OUT)
         vector_step(1)
+        second_z(G_IN)
         second_link(G_QKV)
         second_link(G_O)
-        second_z(G_IN)
         vector_step(2)
         first_z(G_QKV)
         first_z(G_O)
@@ -685,7 +684,6 @@
         pltpu.VMEM((width, seq_len), BF),
         pltpu.VMEM((ff, seq_len), BF),
         pltpu.VMEM((ff, seq_len), BF),
-        pltpu.VMEM((width, seq_len), F32),
         pltpu.VMEM((width, seq_len), F32),
         pltpu.VMEM((width, seq_len), BF),
         pltpu.VMEM((width, seq_len), BF),

time: 137 us -> 133 us (0.971)
  Pallas kernels: 136 us -> 132 us
    pallas_call x1, Pallas kernels: 132 us -> 128 us  [body(): pl.pallas_call(functools.partial(layer_kernel, (batch_count, seq_count, b...]
where the time goes in v4:
time: 133 us; the launch traced here: 132 us
  Pallas kernels  132 us (99%)
    pallas_call x1, Pallas kernels, body(): pl.pallas_call(functools.partial(layer_kernel, (batch_count, seq_count, b...  128 us
    pallas_call x1, Pallas kernels, deliver(): pl.pallas_call(deliver_kernel, out_shape=tuple(shapes) + vectors, in_spec...  3.29 us

profile of v4, /device:TPU:0, one launch (start us, length us, event | category | flops | bytes accessed | tf_op | source)
XLA Modules:
  0.0 132.5 jit_solution(18424683925116916800)
XLA Ops:
  0.7 128.3 %encoder_layer.1 = (bf16[4,128,768]{2,1,0:T(8,128)(2,1)}, bf16[4,128,768]{2,1,0:T(8,128)(2,1)}, f32[4,768]{1,0:T(4,128)}, f32[16,768]{1,0:T(8,128)}, f32[384,192...) custom-call(bf16[4,128,768]{2,1,0:T(8,128)(2,1)} %refs_0_.1, ...), custom_call_target="tpu_custom_call" | custom-call | tf_op jit(solution)/shard_map/encoder_layer/pallas_call | solution.py:727
  129.0 3.3 %deliver.1 = (bf16[4,128,768]{2,1,0:T(8,128)(2,1)}, bf16[4,128,768]{2,1,0:T(8,128)(2,1)}, f32[4,768]{1,0:T(4,128)}, f32[192,384]{1,0:T(8,128)}, f32[96,768]{1,0:...) custom-call(bf16[4,128,768]{2,1,0:T(8,128)(2,1)} %get-tuple-element., ...), custom_call_target="tpu_custom_call" | custom-call | tf_op jit(solution)/shard_map/deliver/pallas_call | solution.py:606

commit v5 on v4

--- a/solution.py
+++ b/solution.py
@@ -178,7 +178,7 @@
         att_t[head_rows(h, 0), :] = (nn(qkv_t[head_rows(h, 2), :], weights_low) * inverse).astype(BF)
         return carry
 
-    lax.fori_loop(0, H, attend, 0)
+    lax.fori_loop(0, H, attend, 0, unroll=4)
 
     loads[1].wait()
     summed = x_t[...].astype(F32) + (tn(w_o[...], att_t[...]) + column(V_BO))

time: 133 us -> 132 us (level)
  Pallas kernels: 132 us -> 130 us
    pallas_call x1, Pallas kernels: 128 us -> 127 us  [body(): pl.pallas_call(functools.partial(layer_kernel, (batch_count, seq_count, b...]
where the time goes in v5:
time: 132 us; the launch traced here: 131 us
  Pallas kernels  130 us (98%)
    pallas_call x1, Pallas kernels, body(): pl.pallas_call(functools.partial(layer_kernel, (batch_count, seq_count, b...  127 us
    pallas_call x1, Pallas kernels, deliver(): pl.pallas_call(deliver_kernel, out_shape=tuple(shapes) + vectors, in_spec...  3.29 us

profile of v5, /device:TPU:0, one launch (start us, length us, event | category | flops | bytes accessed | tf_op | source)
XLA Modules:
  0.0 130.8 jit_solution(9649910566783282289)
XLA Ops:
  0.7 126.7 %encoder_layer.1 = (bf16[4,128,768]{2,1,0:T(8,128)(2,1)}, bf16[4,128,768]{2,1,0:T(8,128)(2,1)}, f32[4,768]{1,0:T(4,128)}, f32[16,768]{1,0:T(8,128)}, f32[384,192...) custom-call(bf16[4,128,768]{2,1,0:T(8,128)(2,1)} %refs_0_.1, ...), custom_call_target="tpu_custom_call" | custom-call | tf_op jit(solution)/shard_map/encoder_layer/pallas_call | solution.py:727
  127.3 3.3 %deliver.1 = (bf16[4,128,768]{2,1,0:T(8,128)(2,1)}, bf16[4,128,768]{2,1,0:T(8,128)(2,1)}, f32[4,768]{1,0:T(4,128)}, f32[192,384]{1,0:T(8,128)}, f32[96,768]{1,0:...) custom-call(bf16[4,128,768]{2,1,0:T(8,128)(2,1)} %get-tuple-element., ...), custom_call_target="tpu_custom_call" | custom-call | tf_op jit(solution)/shard_map/deliver/pallas_call | solution.py:606

commit v6 on v5

--- a/solution.py
+++ b/solution.py
@@ -178,7 +178,7 @@
         att_t[head_rows(h, 0), :] = (nn(qkv_t[head_rows(h, 2), :], weights_low) * inverse).astype(BF)
         return carry
 
-    lax.fori_loop(0, H, attend, 0, unroll=4)
+    lax.fori_loop(0, H, attend, 0, unroll=6)
 
     loads[1].wait()
     summed = x_t[...].astype(F32) + (tn(w_o[...], att_t[...]) + column(V_BO))

time: 132 us -> 132 us (level)
  no operation moved by 1% of the time
where the time goes in v6:
time: 132 us; the launch traced here: 131 us
  Pallas kernels  130 us (98%)
    pallas_call x1, Pallas kernels, body(): pl.pallas_call(functools.partial(layer_kernel, (batch_count, seq_count, b...  126 us
    pallas_call x1, Pallas kernels, deliver(): pl.pallas_call(deliver_kernel, out_shape=tuple(shapes) + vectors, in_spec...  3.29 us

profile of v6, /device:TPU:0, one launch (start us, length us, event | category | flops | bytes accessed | tf_op | source)
XLA Modules:
  0.0 130.6 jit_solution(12109187682343463421)
XLA Ops:
  0.7 126.4 %encoder_layer.1 = (bf16[4,128,768]{2,1,0:T(8,128)(2,1)}, bf16[4,128,768]{2,1,0:T(8,128)(2,1)}, f32[4,768]{1,0:T(4,128)}, f32[16,768]{1,0:T(8,128)}, f32[384,192...) custom-call(bf16[4,128,768]{2,1,0:T(8,128)(2,1)} %refs_0_.1, ...), custom_call_target="tpu_custom_call" | custom-call | tf_op jit(solution)/shard_map/encoder_layer/pallas_call | solution.py:727
  127.1 3.3 %deliver.1 = (bf16[4,128,768]{2,1,0:T(8,128)(2,1)}, bf16[4,128,768]{2,1,0:T(8,128)(2,1)}, f32[4,768]{1,0:T(4,128)}, f32[192,384]{1,0:T(8,128)}, f32[96,768]{1,0:...) custom-call(bf16[4,128,768]{2,1,0:T(8,128)(2,1)} %get-tuple-element., ...), custom_call_target="tpu_custom_call" | custom-call | tf_op jit(solution)/shard_map/deliver/pallas_call | solution.py:606
